TPU v7x, 256 devices: a whole 4x4x8 slice. The times are simulated.
256 devices in a mesh: inst: 64 (over x, y_lo, z), head: 4 (over y_hi, core).
Axes of the slice: x: 4, y: 4 (y_hi: 2, y_lo: 2; y = y_hi * 2 + y_lo), z: 8, core: 2. Of those that a mesh axis runs over, the one named last changes fastest.
Arguments:
- queries: bfloat16 [16384, 8192], P('inst', 'head'), may hold values from -256 to 256
- keys: bfloat16 [16384, 1024], P('inst', 'head'), may hold values from -6 to 6
- values: bfloat16 [16384, 1024], P('inst', 'head'), may hold values from -6 to 6
- segments: int32 [16384], P('inst'), may hold values from 0 to 5, never falling along the last dimension, each value on 1 to 5120 neighbouring positions
- owners: int32 [16384, 1], P('inst'), may hold values from 0 to 63; in each aligned block of 256 rows (0 to 255, 256 to 511, ...) at most 8 rows name the same one
Outputs:
- attended: bfloat16 [16384, 8192], P('inst', 'head')
- cache: bfloat16 [32768, 2048], P('inst')
Inputs may be any that keep to these rules, and one draw needn't show every extreme that they name: `segments`: requests lie in order; each has 1 to 5120 consecutive tokens, one exactly 5120. `owners`: of the 256 tokens of one index of inst, at most 8 name one owner; some owner is named exactly 8 times.
All inputs are finite; a program needn't handle non-finite values.
Results may differ from a plain program's by a relative error of at most 0.006.
Values may be sent and summed in bfloat16 or wider, within the bound.
A program may use at most 128 MiB of HBM per device.

v0:
```python
import jax
import jax.numpy as jnp
from jax import lax
from jax.sharding import PartitionSpec as P

Q_HEADS = 64
KV_HEADS = 8
HEAD_FEATURES = 128


def passed_along(shard, axis, by):
    devices = lax.axis_size(axis)
    pairs = [(i, i + by) for i in range(devices) if 0 <= i + by < devices]
    return lax.ppermute(shard, axis, pairs)


def on_device(queries, keys, values, segments, owners):
    rows = queries.shape[0]
    key_value_width = keys.shape[1]
    group_count = key_value_width // HEAD_FEATURES
    ratio = Q_HEADS // KV_HEADS
    count = lax.axis_size("inst")
    index = lax.axis_index("inst")
    total_rows = rows * count
    reach = total_rows * 5 // 16
    first = index * rows
    qpos = first + jnp.arange(rows, dtype=jnp.int32)
    qgrid = queries.reshape(rows, group_count, ratio, HEAD_FEATURES)
    local_rows = jnp.concatenate([keys, values], axis=1)
    every_seg = lax.all_gather(segments, "inst", axis=0, tiled=True)
    own_seg = lax.dynamic_slice_in_dim(every_seg, first, rows, 0)
    scale = HEAD_FEATURES ** (-0.5)

    def update(carry, block_tile, kstart):
        extent_total = block_tile.shape[0]
        kmat = block_tile[:, :key_value_width].reshape(extent_total, group_count, HEAD_FEATURES)
        value_matrix = block_tile[:, key_value_width:].reshape(
            extent_total, group_count, HEAD_FEATURES
        )
        kpos = kstart + jnp.arange(extent_total, dtype=jnp.int32)
        kseg = jnp.take(every_seg, jnp.clip(kpos, 0, total_rows - 1), axis=0)
        visible = (
            (own_seg[:, None] == kseg[None, :])
            & (kpos[None, :] <= qpos[:, None])
            & (kpos[None, :] >= 0)
        )
        visible = visible[:, None, None, :]
        scores = (
            jnp.einsum("tgra,sga->tgrs", qgrid, kmat, preferred_element_type=jnp.float32) * scale
        )
        scores = jnp.where(visible, scores, jnp.float32(-1e30))
        peak, total, summed = carry
        newpeak = jnp.maximum(peak, jnp.max(scores, axis=-1))
        weight_probs = jnp.where(visible, jnp.exp(scores - newpeak[..., None]), jnp.float32(0.0))
        factor = jnp.exp(peak - newpeak)
        total = total * factor + jnp.sum(weight_probs, axis=-1)
        summed = summed * factor[..., None] + jnp.einsum(
            "oyce,eyk->oyck",
            weight_probs.astype(jnp.bfloat16),
            value_matrix,
            preferred_element_type=jnp.float32,
        )
        return (newpeak, total, summed)

    def attend(carry, piece, start):
        extent_total = piece.shape[0]
        step = extent_total

        def inner(turn, state):
            return update(state, piece, start + turn * step)

        def run(state):
            return lax.fori_loop(0, extent_total // step, inner, state)

        useful = (start <= first + rows - 1) & (start + extent_total - 1 >= first - reach)
        return lax.cond(useful, run, lambda state: state, carry)

    empty = (
        jnp.full((rows, group_count, ratio), -1e30, jnp.float32),
        jnp.zeros((rows, group_count, ratio), jnp.float32),
        jnp.zeros((rows, group_count, ratio, HEAD_FEATURES), jnp.float32),
    )
    steps = min(reach // rows + 1, count - 1)
    start_state = attend(empty, local_rows, first)

    def turn_near(turn, state):
        carry, moving = state
        moving = passed_along(moving, "inst", 1)
        return (attend(carry, moving, first - (turn + 1) * rows), moving)

    final, unused_rows = lax.fori_loop(0, steps, turn_near, (start_state, local_rows))
    peak, total, summed = final
    attended = (
        (summed / total[..., None])
        .astype(jnp.bfloat16)
        .reshape(rows, group_count * ratio * HEAD_FEATURES)
    )
    source_rows = lax.all_gather(local_rows, "head", axis=1, tiled=True)
    slot_size = 2 * rows // count
    dest = owners[:, 0]
    onehot = (dest[:, None] == jnp.arange(count, dtype=jnp.int32)[None, :]).astype(jnp.int32)
    slot = jnp.sum(onehot * (jnp.cumsum(onehot, axis=0) - onehot), axis=1)
    target = dest * slot_size + slot
    placing = (jnp.arange(count * slot_size, dtype=jnp.int32)[:, None] == target[None, :]).astype(
        jnp.bfloat16
    )
    outgoing = jnp.dot(placing, source_rows, preferred_element_type=jnp.float32).astype(
        jnp.bfloat16
    )
    outgoing = outgoing.reshape(count, slot_size, source_rows.shape[1])
    received = lax.all_to_all(outgoing, "inst", split_axis=0, concat_axis=0, tiled=True)
    received = received.reshape(count * slot_size, source_rows.shape[1])
    return (attended, received)


def solution(mesh):
    return jax.shard_map(
        on_device,
        mesh=mesh,
        in_specs=(
            P("inst", "head"),
            P("inst", "head"),
            P("inst", "head"),
            P("inst"),
            P("inst", None),
        ),
        out_specs=(P("inst", "head"), P("inst", None)),
        check_vma=False,
    )
```

profile of v0, /device:TPU:6, one launch (start us, length us, event | category | flops | bytes accessed | tf_op | source)
XLA Modules:
  0.0 695.0 jit_solution(6385321566854353488)
XLA Ops:
  13.0 23.7 %all-gather.3.cloned.1.call-done = bf16[256,2048]{0,1:T(8,128)(2,1)} async-done(((bf16[256,512]{0,1:T(8,128)(2,1)}), bf16[256,2048]{0,1:T(8,128)(2,1)}) %all-gather.3.cloned.1.call-update) | async-done | bytes 1048592 | tf_op jit(solution)/shard_map/all_gather | solution.py:98
  40.0 11.1 %all-to-all-start = ((bf16[64,8,2048]{2,1,0:T(8,128)(2,1)}), bf16[64,8,2048]{2,1,0:T(8,128)(2,1)}, u32[]{:S(2)}, u32[]{:S(2)}) async-start(bf16[64,8,2048]{2,1,0:T(8,128)(2,1)} %fusion.38), calls=%async_computation | async-start | bytes 4194304 | tf_op jit(solution)/shard_map/all_to_all | solution.py:111
  52.3 171.9 %all-gather = s32[64,1,256]{2,1,0:T(1,128)S(1)} all-gather(s32[1,1,256]{2,1,0:T(1,128)S(1)} %bitcast.93), channel_id=1, replica_groups=mesh['inst'=64,'head'=4] {'inst'}, dimensions={0}, use_global_device_ids=true | all-gather | bytes 66560 | tf_op jit(solution)/shard_map/all_gather | solution.py:30
  224.3 12.5 %conditional.2 = (f32[256,2,8]{0,2,1:T(8,128)}, f32[256,2,8]{0,2,1:T(8,128)S(1)}, f32[256,2,8,128]{3,0,2,1:T(8,128)}) conditional(s32[]{:T(128)} %convert_element_type.39, () %tuple.61, (s32[256]{0:T(256)S(1)}, s32[]{:T(128)}, s32[16384]{0:T(1024)S(1)}, s32[]{:T(128)}, bf16[256,256]{1,0:T(8,128)(2,1)S(1)}, ...), branch_computations={%region_0.0_spmd, %region_1.5_spmd} | conditional | flops 551310592 | bytes 33753668 | solution.py:76
  231.6 5.2 bitcast_add_fusion
  236.8 444.4 %while.32 = (s32[]{:T(128)}, f32[256,2,8]{0,2,1:T(8,128)}, f32[256,2,8]{0,2,1:T(8,128)S(1)}, f32[256,2,8,128]{3,0,2,1:T(8,128)}, bf16[256,512]{0,1:T(8,128)(2,1)...) while((s32[]{:T(128)}, f32[256,2,8]{0,2,1:T(8,128)}, ...), condition=%wide.region_9.11_spmd.clone.clone, body=%wide.region_4.10_spmd.clone.clone.sunk | while | flops 551826688 | bytes 20729732 | solution.py:91
  239.5 8.5 %collective-permute-done = bf16[256,512]{0,1:T(8,128)(2,1)S(1)} collective-permute-done((bf16[256,512]{0,1:T(8,128)(2,1)S(1)}, bf16[256,512]{0,1:T(8,128)(2,1)S(1)}, u32[]{:S(2)}, u32[]{:S(2)}) %collective-permute-start) | collective-permute-done | bytes 262176 | tf_op jit(solution)/shard_map/while/body/eval_jaxpr/ppermute | solution.py:14
  248.0 9.9 %conditional.6 = ((f32[256,2,8]{0,2,1:T(8,128)}, f32[256,2,8]{0,2,1:T(8,128)S(1)}, f32[256,2,8,128]{3,0,2,1:T(8,128)})) conditional(s32[]{:T(128)} %convert_element_type.61, (f32[256,2,8]{0,2,1:T(8,128)}, f32[256,2,8]{0,2,1:T(8,128)S(1)}, f32[256,2,8,128]{3,0,2,1:T(8,128)}) %tuple.96, (s32[256]{0:T(256)S(1)}, s32[]{:T(128)}, s32[16384]{0:T(1024)S(1)}, ...), branch_computations={%region_5.6_spmd, %region_6.9_spmd} | conditional | flops 551826688 | bytes 19155504 | solution.py:76
  254.0 4.0 bitcast_add_fusion.1
  260.0 9.3 %collective-permute-done = bf16[256,512]{0,1:T(8,128)(2,1)S(1)} collective-permute-done((bf16[256,512]{0,1:T(8,128)(2,1)S(1)}, bf16[256,512]{0,1:T(8,128)(2,1)S(1)}, u32[]{:S(2)}, u32[]{:S(2)}) %collective-permute-start) | collective-permute-done | bytes 262176 | tf_op jit(solution)/shard_map/while/body/eval_jaxpr/ppermute | solution.py:14
  269.3 9.9 %conditional.6 = ((f32[256,2,8]{0,2,1:T(8,128)}, f32[256,2,8]{0,2,1:T(8,128)S(1)}, f32[256,2,8,128]{3,0,2,1:T(8,128)})) conditional(s32[]{:T(128)} %convert_element_type.61, (f32[256,2,8]{0,2,1:T(8,128)}, f32[256,2,8]{0,2,1:T(8,128)S(1)}, f32[256,2,8,128]{3,0,2,1:T(8,128)}) %tuple.96, (s32[256]{0:T(256)S(1)}, s32[]{:T(128)}, s32[16384]{0:T(1024)S(1)}, ...), branch_computations={%region_5.6_spmd, %region_6.9_spmd} | conditional | flops 551826688 | bytes 19155504 | solution.py:76
  275.2 4.0 bitcast_add_fusion.1
  281.2 9.3 %collective-permute-done = bf16[256,512]{0,1:T(8,128)(2,1)S(1)} collective-permute-done((bf16[256,512]{0,1:T(8,128)(2,1)S(1)}, bf16[256,512]{0,1:T(8,128)(2,1)S(1)}, u32[]{:S(2)}, u32[]{:S(2)}) %collective-permute-start) | collective-permute-done | bytes 262176 | tf_op jit(solution)/shard_map/while/body/eval_jaxpr/ppermute | solution.py:14
  290.6 9.9 %conditional.6 = ((f32[256,2,8]{0,2,1:T(8,128)}, f32[256,2,8]{0,2,1:T(8,128)S(1)}, f32[256,2,8,128]{3,0,2,1:T(8,128)})) conditional(s32[]{:T(128)} %convert_element_type.61, (f32[256,2,8]{0,2,1:T(8,128)}, f32[256,2,8]{0,2,1:T(8,128)S(1)}, f32[256,2,8,128]{3,0,2,1:T(8,128)}) %tuple.96, (s32[256]{0:T(256)S(1)}, s32[]{:T(128)}, s32[16384]{0:T(1024)S(1)}, ...), branch_computations={%region_5.6_spmd, %region_6.9_spmd} | conditional | flops 551826688 | bytes 19155504 | solution.py:76
  296.5 4.0 bitcast_add_fusion.1
  302.5 9.3 %collective-permute-done = bf16[256,512]{0,1:T(8,128)(2,1)S(1)} collective-permute-done((bf16[256,512]{0,1:T(8,128)(2,1)S(1)}, bf16[256,512]{0,1:T(8,128)(2,1)S(1)}, u32[]{:S(2)}, u32[]{:S(2)}) %collective-permute-start) | collective-permute-done | bytes 262176 | tf_op jit(solution)/shard_map/while/body/eval_jaxpr/ppermute | solution.py:14
  311.8 9.9 %conditional.6 = ((f32[256,2,8]{0,2,1:T(8,128)}, f32[256,2,8]{0,2,1:T(8,128)S(1)}, f32[256,2,8,128]{3,0,2,1:T(8,128)})) conditional(s32[]{:T(128)} %convert_element_type.61, (f32[256,2,8]{0,2,1:T(8,128)}, f32[256,2,8]{0,2,1:T(8,128)S(1)}, f32[256,2,8,128]{3,0,2,1:T(8,128)}) %tuple.96, (s32[256]{0:T(256)S(1)}, s32[]{:T(128)}, s32[16384]{0:T(1024)S(1)}, ...), branch_computations={%region_5.6_spmd, %region_6.9_spmd} | conditional | flops 551826688 | bytes 19155504 | solution.py:76
  317.8 4.0 bitcast_add_fusion.1
  323.7 9.3 %collective-permute-done = bf16[256,512]{0,1:T(8,128)(2,1)S(1)} collective-permute-done((bf16[256,512]{0,1:T(8,128)(2,1)S(1)}, bf16[256,512]{0,1:T(8,128)(2,1)S(1)}, u32[]{:S(2)}, u32[]{:S(2)}) %collective-permute-start) | collective-permute-done | bytes 262176 | tf_op jit(solution)/shard_map/while/body/eval_jaxpr/ppermute | solution.py:14
  333.1 9.9 %conditional.6 = ((f32[256,2,8]{0,2,1:T(8,128)}, f32[256,2,8]{0,2,1:T(8,128)S(1)}, f32[256,2,8,128]{3,0,2,1:T(8,128)})) conditional(s32[]{:T(128)} %convert_element_type.61, (f32[256,2,8]{0,2,1:T(8,128)}, f32[256,2,8]{0,2,1:T(8,128)S(1)}, f32[256,2,8,128]{3,0,2,1:T(8,128)}) %tuple.96, (s32[256]{0:T(256)S(1)}, s32[]{:T(128)}, s32[16384]{0:T(1024)S(1)}, ...), branch_computations={%region_5.6_spmd, %region_6.9_spmd} | conditional | flops 551826688 | bytes 19155504 | solution.py:76
  339.0 4.0 bitcast_add_fusion.1
  345.0 9.3 %collective-permute-done = bf16[256,512]{0,1:T(8,128)(2,1)S(1)} collective-permute-done((bf16[256,512]{0,1:T(8,128)(2,1)S(1)}, bf16[256,512]{0,1:T(8,128)(2,1)S(1)}, u32[]{:S(2)}, u32[]{:S(2)}) %collective-permute-start) | collective-permute-done | bytes 262176 | tf_op jit(solution)/shard_map/while/body/eval_jaxpr/ppermute | solution.py:14
  354.3 9.9 %conditional.6 = ((f32[256,2,8]{0,2,1:T(8,128)}, f32[256,2,8]{0,2,1:T(8,128)S(1)}, f32[256,2,8,128]{3,0,2,1:T(8,128)})) conditional(s32[]{:T(128)} %convert_element_type.61, (f32[256,2,8]{0,2,1:T(8,128)}, f32[256,2,8]{0,2,1:T(8,128)S(1)}, f32[256,2,8,128]{3,0,2,1:T(8,128)}) %tuple.96, (s32[256]{0:T(256)S(1)}, s32[]{:T(128)}, s32[16384]{0:T(1024)S(1)}, ...), branch_computations={%region_5.6_spmd, %region_6.9_spmd} | conditional | flops 551826688 | bytes 19155504 | solution.py:76
  360.3 4.0 bitcast_add_fusion.1
  366.2 9.3 %collective-permute-done = bf16[256,512]{0,1:T(8,128)(2,1)S(1)} collective-permute-done((bf16[256,512]{0,1:T(8,128)(2,1)S(1)}, bf16[256,512]{0,1:T(8,128)(2,1)S(1)}, u32[]{:S(2)}, u32[]{:S(2)}) %collective-permute-start) | collective-permute-done | bytes 262176 | tf_op jit(solution)/shard_map/while/body/eval_jaxpr/ppermute | solution.py:14
  375.6 9.9 %conditional.6 = ((f32[256,2,8]{0,2,1:T(8,128)}, f32[256,2,8]{0,2,1:T(8,128)S(1)}, f32[256,2,8,128]{3,0,2,1:T(8,128)})) conditional(s32[]{:T(128)} %convert_element_type.61, (f32[256,2,8]{0,2,1:T(8,128)}, f32[256,2,8]{0,2,1:T(8,128)S(1)}, f32[256,2,8,128]{3,0,2,1:T(8,128)}) %tuple.96, (s32[256]{0:T(256)S(1)}, s32[]{:T(128)}, s32[16384]{0:T(1024)S(1)}, ...), branch_computations={%region_5.6_spmd, %region_6.9_spmd} | conditional | flops 551826688 | bytes 19155504 | solution.py:76
  381.5 4.0 bitcast_add_fusion.1
  387.5 9.3 %collective-permute-done = bf16[256,512]{0,1:T(8,128)(2,1)S(1)} collective-permute-done((bf16[256,512]{0,1:T(8,128)(2,1)S(1)}, bf16[256,512]{0,1:T(8,128)(2,1)S(1)}, u32[]{:S(2)}, u32[]{:S(2)}) %collective-permute-start) | collective-permute-done | bytes 262176 | tf_op jit(solution)/shard_map/while/body/eval_jaxpr/ppermute | solution.py:14
  396.8 9.9 %conditional.6 = ((f32[256,2,8]{0,2,1:T(8,128)}, f32[256,2,8]{0,2,1:T(8,128)S(1)}, f32[256,2,8,128]{3,0,2,1:T(8,128)})) conditional(s32[]{:T(128)} %convert_element_type.61, (f32[256,2,8]{0,2,1:T(8,128)}, f32[256,2,8]{0,2,1:T(8,128)S(1)}, f32[256,2,8,128]{3,0,2,1:T(8,128)}) %tuple.96, (s32[256]{0:T(256)S(1)}, s32[]{:T(128)}, s32[16384]{0:T(1024)S(1)}, ...), branch_computations={%region_5.6_spmd, %region_6.9_spmd} | conditional | flops 551826688 | bytes 19155504 | solution.py:76
  408.8 9.8 %collective-permute-done = bf16[256,512]{0,1:T(8,128)(2,1)S(1)} collective-permute-done((bf16[256,512]{0,1:T(8,128)(2,1)S(1)}, bf16[256,512]{0,1:T(8,128)(2,1)S(1)}, u32[]{:S(2)}, u32[]{:S(2)}) %collective-permute-start) | collective-permute-done | bytes 262176 | tf_op jit(solution)/shard_map/while/body/eval_jaxpr/ppermute | solution.py:14
  418.5 9.9 %conditional.6 = ((f32[256,2,8]{0,2,1:T(8,128)}, f32[256,2,8]{0,2,1:T(8,128)S(1)}, f32[256,2,8,128]{3,0,2,1:T(8,128)})) conditional(s32[]{:T(128)} %convert_element_type.61, (f32[256,2,8]{0,2,1:T(8,128)}, f32[256,2,8]{0,2,1:T(8,128)S(1)}, f32[256,2,8,128]{3,0,2,1:T(8,128)}) %tuple.96, (s32[256]{0:T(256)S(1)}, s32[]{:T(128)}, s32[16384]{0:T(1024)S(1)}, ...), branch_computations={%region_5.6_spmd, %region_6.9_spmd} | conditional | flops 551826688 | bytes 19155504 | solution.py:76
  424.5 4.0 bitcast_add_fusion.1
  430.5 10.9 %collective-permute-done = bf16[256,512]{0,1:T(8,128)(2,1)S(1)} collective-permute-done((bf16[256,512]{0,1:T(8,128)(2,1)S(1)}, bf16[256,512]{0,1:T(8,128)(2,1)S(1)}, u32[]{:S(2)}, u32[]{:S(2)}) %collective-permute-start) | collective-permute-done | bytes 262176 | tf_op jit(solution)/shard_map/while/body/eval_jaxpr/ppermute | solution.py:14
  441.3 9.9 %conditional.6 = ((f32[256,2,8]{0,2,1:T(8,128)}, f32[256,2,8]{0,2,1:T(8,128)S(1)}, f32[256,2,8,128]{3,0,2,1:T(8,128)})) conditional(s32[]{:T(128)} %convert_element_type.61, (f32[256,2,8]{0,2,1:T(8,128)}, f32[256,2,8]{0,2,1:T(8,128)S(1)}, f32[256,2,8,128]{3,0,2,1:T(8,128)}) %tuple.96, (s32[256]{0:T(256)S(1)}, s32[]{:T(128)}, s32[16384]{0:T(1024)S(1)}, ...), branch_computations={%region_5.6_spmd, %region_6.9_spmd} | conditional | flops 551826688 | bytes 19155504 | solution.py:76
  453.3 12.0 %collective-permute-done = bf16[256,512]{0,1:T(8,128)(2,1)S(1)} collective-permute-done((bf16[256,512]{0,1:T(8,128)(2,1)S(1)}, bf16[256,512]{0,1:T(8,128)(2,1)S(1)}, u32[]{:S(2)}, u32[]{:S(2)}) %collective-permute-start) | collective-permute-done | bytes 262176 | tf_op jit(solution)/shard_map/while/body/eval_jaxpr/ppermute | solution.py:14
  465.3 9.9 %conditional.6 = ((f32[256,2,8]{0,2,1:T(8,128)}, f32[256,2,8]{0,2,1:T(8,128)S(1)}, f32[256,2,8,128]{3,0,2,1:T(8,128)})) conditional(s32[]{:T(128)} %convert_element_type.61, (f32[256,2,8]{0,2,1:T(8,128)}, f32[256,2,8]{0,2,1:T(8,128)S(1)}, f32[256,2,8,128]{3,0,2,1:T(8,128)}) %tuple.96, (s32[256]{0:T(256)S(1)}, s32[]{:T(128)}, s32[16384]{0:T(1024)S(1)}, ...), branch_computations={%region_5.6_spmd, %region_6.9_spmd} | conditional | flops 551826688 | bytes 19155504 | solution.py:76
  471.3 4.0 bitcast_add_fusion.1
  477.2 11.3 %collective-permute-done = bf16[256,512]{0,1:T(8,128)(2,1)S(1)} collective-permute-done((bf16[256,512]{0,1:T(8,128)(2,1)S(1)}, bf16[256,512]{0,1:T(8,128)(2,1)S(1)}, u32[]{:S(2)}, u32[]{:S(2)}) %collective-permute-start) | collective-permute-done | bytes 262176 | tf_op jit(solution)/shard_map/while/body/eval_jaxpr/ppermute | solution.py:14
  488.5 9.9 %conditional.6 = ((f32[256,2,8]{0,2,1:T(8,128)}, f32[256,2,8]{0,2,1:T(8,128)S(1)}, f32[256,2,8,128]{3,0,2,1:T(8,128)})) conditional(s32[]{:T(128)} %convert_element_type.61, (f32[256,2,8]{0,2,1:T(8,128)}, f32[256,2,8]{0,2,1:T(8,128)S(1)}, f32[256,2,8,128]{3,0,2,1:T(8,128)}) %tuple.96, (s32[256]{0:T(256)S(1)}, s32[]{:T(128)}, s32[16384]{0:T(1024)S(1)}, ...), branch_computations={%region_5.6_spmd, %region_6.9_spmd} | conditional | flops 551826688 | bytes 19155504 | solution.py:76
  494.5 4.0 bitcast_add_fusion.1
  500.4 10.4 %collective-permute-done = bf16[256,512]{0,1:T(8,128)(2,1)S(1)} collective-permute-done((bf16[256,512]{0,1:T(8,128)(2,1)S(1)}, bf16[256,512]{0,1:T(8,128)(2,1)S(1)}, u32[]{:S(2)}, u32[]{:S(2)}) %collective-permute-start) | collective-permute-done | bytes 262176 | tf_op jit(solution)/shard_map/while/body/eval_jaxpr/ppermute | solution.py:14
  510.9 9.9 %conditional.6 = ((f32[256,2,8]{0,2,1:T(8,128)}, f32[256,2,8]{0,2,1:T(8,128)S(1)}, f32[256,2,8,128]{3,0,2,1:T(8,128)})) conditional(s32[]{:T(128)} %convert_element_type.61, (f32[256,2,8]{0,2,1:T(8,128)}, f32[256,2,8]{0,2,1:T(8,128)S(1)}, f32[256,2,8,128]{3,0,2,1:T(8,128)}) %tuple.96, (s32[256]{0:T(256)S(1)}, s32[]{:T(128)}, s32[16384]{0:T(1024)S(1)}, ...), branch_computations={%region_5.6_spmd, %region_6.9_spmd} | conditional | flops 551826688 | bytes 19155504 | solution.py:76
  516.8 4.0 bitcast_add_fusion.1
  522.8 9.5 %collective-permute-done = bf16[256,512]{0,1:T(8,128)(2,1)S(1)} collective-permute-done((bf16[256,512]{0,1:T(8,128)(2,1)S(1)}, bf16[256,512]{0,1:T(8,128)(2,1)S(1)}, u32[]{:S(2)}, u32[]{:S(2)}) %collective-permute-start) | collective-permute-done | bytes 262176 | tf_op jit(solution)/shard_map/while/body/eval_jaxpr/ppermute | solution.py:14
  532.3 9.9 %conditional.6 = ((f32[256,2,8]{0,2,1:T(8,128)}, f32[256,2,8]{0,2,1:T(8,128)S(1)}, f32[256,2,8,128]{3,0,2,1:T(8,128)})) conditional(s32[]{:T(128)} %convert_element_type.61, (f32[256,2,8]{0,2,1:T(8,128)}, f32[256,2,8]{0,2,1:T(8,128)S(1)}, f32[256,2,8,128]{3,0,2,1:T(8,128)}) %tuple.96, (s32[256]{0:T(256)S(1)}, s32[]{:T(128)}, s32[16384]{0:T(1024)S(1)}, ...), branch_computations={%region_5.6_spmd, %region_6.9_spmd} | conditional | flops 551826688 | bytes 19155504 | solution.py:76
  538.3 4.0 bitcast_add_fusion.1
  544.3 9.3 %collective-permute-done = bf16[256,512]{0,1:T(8,128)(2,1)S(1)} collective-permute-done((bf16[256,512]{0,1:T(8,128)(2,1)S(1)}, bf16[256,512]{0,1:T(8,128)(2,1)S(1)}, u32[]{:S(2)}, u32[]{:S(2)}) %collective-permute-start) | collective-permute-done | bytes 262176 | tf_op jit(solution)/shard_map/while/body/eval_jaxpr/ppermute | solution.py:14
  553.6 9.9 %conditional.6 = ((f32[256,2,8]{0,2,1:T(8,128)}, f32[256,2,8]{0,2,1:T(8,128)S(1)}, f32[256,2,8,128]{3,0,2,1:T(8,128)})) conditional(s32[]{:T(128)} %convert_element_type.61, (f32[256,2,8]{0,2,1:T(8,128)}, f32[256,2,8]{0,2,1:T(8,128)S(1)}, f32[256,2,8,128]{3,0,2,1:T(8,128)}) %tuple.96, (s32[256]{0:T(256)S(1)}, s32[]{:T(128)}, s32[16384]{0:T(1024)S(1)}, ...), branch_computations={%region_5.6_spmd, %region_6.9_spmd} | conditional | flops 551826688 | bytes 19155504 | solution.py:76
  559.5 4.0 bitcast_add_fusion.1
  565.5 9.3 %collective-permute-done = bf16[256,512]{0,1:T(8,128)(2,1)S(1)} collective-permute-done((bf16[256,512]{0,1:T(8,128)(2,1)S(1)}, bf16[256,512]{0,1:T(8,128)(2,1)S(1)}, u32[]{:S(2)}, u32[]{:S(2)}) %collective-permute-start) | collective-permute-done | bytes 262176 | tf_op jit(solution)/shard_map/while/body/eval_jaxpr/ppermute | solution.py:14
  574.9 9.9 %conditional.6 = ((f32[256,2,8]{0,2,1:T(8,128)}, f32[256,2,8]{0,2,1:T(8,128)S(1)}, f32[256,2,8,128]{3,0,2,1:T(8,128)})) conditional(s32[]{:T(128)} %convert_element_type.61, (f32[256,2,8]{0,2,1:T(8,128)}, f32[256,2,8]{0,2,1:T(8,128)S(1)}, f32[256,2,8,128]{3,0,2,1:T(8,128)}) %tuple.96, (s32[256]{0:T(256)S(1)}, s32[]{:T(128)}, s32[16384]{0:T(1024)S(1)}, ...), branch_computations={%region_5.6_spmd, %region_6.9_spmd} | conditional | flops 551826688 | bytes 19155504 | solution.py:76
  580.8 4.0 bitcast_add_fusion.1
  586.8 9.3 %collective-permute-done = bf16[256,512]{0,1:T(8,128)(2,1)S(1)} collective-permute-done((bf16[256,512]{0,1:T(8,128)(2,1)S(1)}, bf16[256,512]{0,1:T(8,128)(2,1)S(1)}, u32[]{:S(2)}, u32[]{:S(2)}) %collective-permute-start) | collective-permute-done | bytes 262176 | tf_op jit(solution)/shard_map/while/body/eval_jaxpr/ppermute | solution.py:14
  596.1 9.9 %conditional.6 = ((f32[256,2,8]{0,2,1:T(8,128)}, f32[256,2,8]{0,2,1:T(8,128)S(1)}, f32[256,2,8,128]{3,0,2,1:T(8,128)})) conditional(s32[]{:T(128)} %convert_element_type.61, (f32[256,2,8]{0,2,1:T(8,128)}, f32[256,2,8]{0,2,1:T(8,128)S(1)}, f32[256,2,8,128]{3,0,2,1:T(8,128)}) %tuple.96, (s32[256]{0:T(256)S(1)}, s32[]{:T(128)}, s32[16384]{0:T(1024)S(1)}, ...), branch_computations={%region_5.6_spmd, %region_6.9_spmd} | conditional | flops 551826688 | bytes 19155504 | solution.py:76
  608.0 9.3 %collective-permute-done = bf16[256,512]{0,1:T(8,128)(2,1)S(1)} collective-permute-done((bf16[256,512]{0,1:T(8,128)(2,1)S(1)}, bf16[256,512]{0,1:T(8,128)(2,1)S(1)}, u32[]{:S(2)}, u32[]{:S(2)}) %collective-permute-start) | collective-permute-done | bytes 262176 | tf_op jit(solution)/shard_map/while/body/eval_jaxpr/ppermute | solution.py:14
  617.3 9.9 %conditional.6 = ((f32[256,2,8]{0,2,1:T(8,128)}, f32[256,2,8]{0,2,1:T(8,128)S(1)}, f32[256,2,8,128]{3,0,2,1:T(8,128)})) conditional(s32[]{:T(128)} %convert_element_type.61, (f32[256,2,8]{0,2,1:T(8,128)}, f32[256,2,8]{0,2,1:T(8,128)S(1)}, f32[256,2,8,128]{3,0,2,1:T(8,128)}) %tuple.96, (s32[256]{0:T(256)S(1)}, s32[]{:T(128)}, s32[16384]{0:T(1024)S(1)}, ...), branch_computations={%region_5.6_spmd, %region_6.9_spmd} | conditional | flops 551826688 | bytes 19155504 | solution.py:76
  623.3 4.0 bitcast_add_fusion.1
  629.3 9.3 %collective-permute-done = bf16[256,512]{0,1:T(8,128)(2,1)S(1)} collective-permute-done((bf16[256,512]{0,1:T(8,128)(2,1)S(1)}, bf16[256,512]{0,1:T(8,128)(2,1)S(1)}, u32[]{:S(2)}, u32[]{:S(2)}) %collective-permute-start) | collective-permute-done | bytes 262176 | tf_op jit(solution)/shard_map/while/body/eval_jaxpr/ppermute | solution.py:14
  638.6 9.9 %conditional.6 = ((f32[256,2,8]{0,2,1:T(8,128)}, f32[256,2,8]{0,2,1:T(8,128)S(1)}, f32[256,2,8,128]{3,0,2,1:T(8,128)})) conditional(s32[]{:T(128)} %convert_element_type.61, (f32[256,2,8]{0,2,1:T(8,128)}, f32[256,2,8]{0,2,1:T(8,128)S(1)}, f32[256,2,8,128]{3,0,2,1:T(8,128)}) %tuple.96, (s32[256]{0:T(256)S(1)}, s32[]{:T(128)}, s32[16384]{0:T(1024)S(1)}, ...), branch_computations={%region_5.6_spmd, %region_6.9_spmd} | conditional | flops 551826688 | bytes 19155504 | solution.py:76
  644.6 4.0 bitcast_add_fusion.1
  650.5 9.3 %collective-permute-done = bf16[256,512]{0,1:T(8,128)(2,1)S(1)} collective-permute-done((bf16[256,512]{0,1:T(8,128)(2,1)S(1)}, bf16[256,512]{0,1:T(8,128)(2,1)S(1)}, u32[]{:S(2)}, u32[]{:S(2)}) %collective-permute-start) | collective-permute-done | bytes 262176 | tf_op jit(solution)/shard_map/while/body/eval_jaxpr/ppermute | solution.py:14
  659.9 9.9 %conditional.6 = ((f32[256,2,8]{0,2,1:T(8,128)}, f32[256,2,8]{0,2,1:T(8,128)S(1)}, f32[256,2,8,128]{3,0,2,1:T(8,128)})) conditional(s32[]{:T(128)} %convert_element_type.61, (f32[256,2,8]{0,2,1:T(8,128)}, f32[256,2,8]{0,2,1:T(8,128)S(1)}, f32[256,2,8,128]{3,0,2,1:T(8,128)}) %tuple.96, (s32[256]{0:T(256)S(1)}, s32[]{:T(128)}, s32[16384]{0:T(1024)S(1)}, ...), branch_computations={%region_5.6_spmd, %region_6.9_spmd} | conditional | flops 551826688 | bytes 19155504 | solution.py:76
  665.8 4.0 bitcast_add_fusion.1
  671.8 9.3 %collective-permute-done = bf16[256,512]{0,1:T(8,128)(2,1)S(1)} collective-permute-done((bf16[256,512]{0,1:T(8,128)(2,1)S(1)}, bf16[256,512]{0,1:T(8,128)(2,1)S(1)}, u32[]{:S(2)}, u32[]{:S(2)}) %collective-permute-start) | collective-permute-done | bytes 262176 | tf_op jit(solution)/shard_map/while/body/eval_jaxpr/ppermute | solution.py:14
  (374 shorter events, 195.9 us)
Async XLA Ops:
  7.2 29.5 %all-gather.3.cloned.1.call-start = ((), (), s32[]{:S(2)}) async-start(), calls=%async_computation.1 | async-start | bytes 1310720 | tf_op jit(solution)/shard_map/all_gather | solution.py:98
  9.2 41.8 %copy-start.1 = (bf16[256,2048]{1,0:T(8,128)(2,1)S(1)}, bf16[256,2048]{1,0:T(8,128)(2,1)}, u32[]{:S(2)}) copy-start(bf16[256,2048]{1,0:T(8,128)(2,1)} %param.13) | copy-start | bytes 3145732
  40.0 12.3 %copy-start.5 = (s32[256]{0:T(256)S(1)}, s32[256]{0:T(256)}, u32[]{:S(2)}) copy-start(s32[256]{0:T(256)} %param.16) | copy-start | bytes 3076
  40.0 184.3 %copy-start.3 = (bf16[256,256]{1,0:T(8,128)(2,1)S(1)}, bf16[256,256]{1,0:T(8,128)(2,1)}, u32[]{:S(2)}) copy-start(bf16[256,256]{1,0:T(8,128)(2,1)} %param.14) | copy-start | bytes 393220
  40.0 184.3 %copy-start.4 = (bf16[256,256]{1,0:T(8,128)(2,1)S(1)}, bf16[256,256]{1,0:T(8,128)(2,1)}, u32[]{:S(2)}) copy-start(bf16[256,256]{1,0:T(8,128)(2,1)} %param.15) | copy-start | bytes 393220
  40.0 645.1 %all-to-all-start = ((bf16[64,8,2048]{2,1,0:T(8,128)(2,1)}), bf16[64,8,2048]{2,1,0:T(8,128)(2,1)}, u32[]{:S(2)}, u32[]{:S(2)}) async-start(bf16[64,8,2048]{2,1,0:T(8,128)(2,1)} %fusion.38), calls=%async_computation | async-start | bytes 4194304 | tf_op jit(solution)/shard_map/all_to_all | solution.py:111
  224.3 12.5 %copy-start.2 = (bf16[256,512]{0,1:T(8,128)(2,1)S(1)}, bf16[256,512]{0,1:T(8,128)(2,1)}, u32[]{:S(2)}) copy-start(bf16[256,512]{0,1:T(8,128)(2,1)} %pad_maximum_fusion) | copy-start | bytes 786436
  227.1 1.9 copy-start
  236.8 11.3 %collective-permute-start = (bf16[256,512]{0,1:T(8,128)(2,1)S(1)}, bf16[256,512]{0,1:T(8,128)(2,1)S(1)}, u32[]{:S(2)}, u32[]{:S(2)}) collective-permute-start(bf16[256,512]{0,1:T(8,128)(2,1)S(1)} %get-tuple-element.781), channel_id=1, source_target_pairs={{0,4},{4,8},{8,12},{12,16},{16,20},{20,24},{24,28},{28,32},{32,36}... | collective-permute-start | bytes 786440 | tf_op jit(solution)/shard_map/while/body/eval_jaxpr/ppermute | solution.py:14
  258.0 11.3 %collective-permute-start = (bf16[256,512]{0,1:T(8,128)(2,1)S(1)}, bf16[256,512]{0,1:T(8,128)(2,1)S(1)}, u32[]{:S(2)}, u32[]{:S(2)}) collective-permute-start(bf16[256,512]{0,1:T(8,128)(2,1)S(1)} %get-tuple-element.781), channel_id=1, source_target_pairs={{0,4},{4,8},{8,12},{12,16},{16,20},{20,24},{24,28},{28,32},{32,36}... | collective-permute-start | bytes 786440 | tf_op jit(solution)/shard_map/while/body/eval_jaxpr/ppermute | solution.py:14
  279.3 11.3 %collective-permute-start = (bf16[256,512]{0,1:T(8,128)(2,1)S(1)}, bf16[256,512]{0,1:T(8,128)(2,1)S(1)}, u32[]{:S(2)}, u32[]{:S(2)}) collective-permute-start(bf16[256,512]{0,1:T(8,128)(2,1)S(1)} %get-tuple-element.781), channel_id=1, source_target_pairs={{0,4},{4,8},{8,12},{12,16},{16,20},{20,24},{24,28},{28,32},{32,36}... | collective-permute-start | bytes 786440 | tf_op jit(solution)/shard_map/while/body/eval_jaxpr/ppermute | solution.py:14
  300.5 11.3 %collective-permute-start = (bf16[256,512]{0,1:T(8,128)(2,1)S(1)}, bf16[256,512]{0,1:T(8,128)(2,1)S(1)}, u32[]{:S(2)}, u32[]{:S(2)}) collective-permute-start(bf16[256,512]{0,1:T(8,128)(2,1)S(1)} %get-tuple-element.781), channel_id=1, source_target_pairs={{0,4},{4,8},{8,12},{12,16},{16,20},{20,24},{24,28},{28,32},{32,36}... | collective-permute-start | bytes 786440 | tf_op jit(solution)/shard_map/while/body/eval_jaxpr/ppermute | solution.py:14
  321.8 11.3 %collective-permute-start = (bf16[256,512]{0,1:T(8,128)(2,1)S(1)}, bf16[256,512]{0,1:T(8,128)(2,1)S(1)}, u32[]{:S(2)}, u32[]{:S(2)}) collective-permute-start(bf16[256,512]{0,1:T(8,128)(2,1)S(1)} %get-tuple-element.781), channel_id=1, source_target_pairs={{0,4},{4,8},{8,12},{12,16},{16,20},{20,24},{24,28},{28,32},{32,36}... | collective-permute-start | bytes 786440 | tf_op jit(solution)/shard_map/while/body/eval_jaxpr/ppermute | solution.py:14
  343.0 11.3 %collective-permute-start = (bf16[256,512]{0,1:T(8,128)(2,1)S(1)}, bf16[256,512]{0,1:T(8,128)(2,1)S(1)}, u32[]{:S(2)}, u32[]{:S(2)}) collective-permute-start(bf16[256,512]{0,1:T(8,128)(2,1)S(1)} %get-tuple-element.781), channel_id=1, source_target_pairs={{0,4},{4,8},{8,12},{12,16},{16,20},{20,24},{24,28},{28,32},{32,36}... | collective-permute-start | bytes 786440 | tf_op jit(solution)/shard_map/while/body/eval_jaxpr/ppermute | solution.py:14
  364.3 11.3 %collective-permute-start = (bf16[256,512]{0,1:T(8,128)(2,1)S(1)}, bf16[256,512]{0,1:T(8,128)(2,1)S(1)}, u32[]{:S(2)}, u32[]{:S(2)}) collective-permute-start(bf16[256,512]{0,1:T(8,128)(2,1)S(1)} %get-tuple-element.781), channel_id=1, source_target_pairs={{0,4},{4,8},{8,12},{12,16},{16,20},{20,24},{24,28},{28,32},{32,36}... | collective-permute-start | bytes 786440 | tf_op jit(solution)/shard_map/while/body/eval_jaxpr/ppermute | solution.py:14
  385.5 11.3 %collective-permute-start = (bf16[256,512]{0,1:T(8,128)(2,1)S(1)}, bf16[256,512]{0,1:T(8,128)(2,1)S(1)}, u32[]{:S(2)}, u32[]{:S(2)}) collective-permute-start(bf16[256,512]{0,1:T(8,128)(2,1)S(1)} %get-tuple-element.781), channel_id=1, source_target_pairs={{0,4},{4,8},{8,12},{12,16},{16,20},{20,24},{24,28},{28,32},{32,36}... | collective-permute-start | bytes 786440 | tf_op jit(solution)/shard_map/while/body/eval_jaxpr/ppermute | solution.py:14
  406.8 11.7 %collective-permute-start = (bf16[256,512]{0,1:T(8,128)(2,1)S(1)}, bf16[256,512]{0,1:T(8,128)(2,1)S(1)}, u32[]{:S(2)}, u32[]{:S(2)}) collective-permute-start(bf16[256,512]{0,1:T(8,128)(2,1)S(1)} %get-tuple-element.781), channel_id=1, source_target_pairs={{0,4},{4,8},{8,12},{12,16},{16,20},{20,24},{24,28},{28,32},{32,36}... | collective-permute-start | bytes 786440 | tf_op jit(solution)/shard_map/while/body/eval_jaxpr/ppermute | solution.py:14
  428.5 12.8 %collective-permute-start = (bf16[256,512]{0,1:T(8,128)(2,1)S(1)}, bf16[256,512]{0,1:T(8,128)(2,1)S(1)}, u32[]{:S(2)}, u32[]{:S(2)}) collective-permute-start(bf16[256,512]{0,1:T(8,128)(2,1)S(1)} %get-tuple-element.781), channel_id=1, source_target_pairs={{0,4},{4,8},{8,12},{12,16},{16,20},{20,24},{24,28},{28,32},{32,36}... | collective-permute-start | bytes 786440 | tf_op jit(solution)/shard_map/while/body/eval_jaxpr/ppermute | solution.py:14
  451.3 14.0 %collective-permute-start = (bf16[256,512]{0,1:T(8,128)(2,1)S(1)}, bf16[256,512]{0,1:T(8,128)(2,1)S(1)}, u32[]{:S(2)}, u32[]{:S(2)}) collective-permute-start(bf16[256,512]{0,1:T(8,128)(2,1)S(1)} %get-tuple-element.781), channel_id=1, source_target_pairs={{0,4},{4,8},{8,12},{12,16},{16,20},{20,24},{24,28},{28,32},{32,36}... | collective-permute-start | bytes 786440 | tf_op jit(solution)/shard_map/while/body/eval_jaxpr/ppermute | solution.py:14
  475.3 13.2 %collective-permute-start = (bf16[256,512]{0,1:T(8,128)(2,1)S(1)}, bf16[256,512]{0,1:T(8,128)(2,1)S(1)}, u32[]{:S(2)}, u32[]{:S(2)}) collective-permute-start(bf16[256,512]{0,1:T(8,128)(2,1)S(1)} %get-tuple-element.781), channel_id=1, source_target_pairs={{0,4},{4,8},{8,12},{12,16},{16,20},{20,24},{24,28},{28,32},{32,36}... | collective-permute-start | bytes 786440 | tf_op jit(solution)/shard_map/while/body/eval_jaxpr/ppermute | solution.py:14
  498.5 12.4 %collective-permute-start = (bf16[256,512]{0,1:T(8,128)(2,1)S(1)}, bf16[256,512]{0,1:T(8,128)(2,1)S(1)}, u32[]{:S(2)}, u32[]{:S(2)}) collective-permute-start(bf16[256,512]{0,1:T(8,128)(2,1)S(1)} %get-tuple-element.781), channel_id=1, source_target_pairs={{0,4},{4,8},{8,12},{12,16},{16,20},{20,24},{24,28},{28,32},{32,36}... | collective-permute-start | bytes 786440 | tf_op jit(solution)/shard_map/while/body/eval_jaxpr/ppermute | solution.py:14
  520.9 11.5 %collective-permute-start = (bf16[256,512]{0,1:T(8,128)(2,1)S(1)}, bf16[256,512]{0,1:T(8,128)(2,1)S(1)}, u32[]{:S(2)}, u32[]{:S(2)}) collective-permute-start(bf16[256,512]{0,1:T(8,128)(2,1)S(1)} %get-tuple-element.781), channel_id=1, source_target_pairs={{0,4},{4,8},{8,12},{12,16},{16,20},{20,24},{24,28},{28,32},{32,36}... | collective-permute-start | bytes 786440 | tf_op jit(solution)/shard_map/while/body/eval_jaxpr/ppermute | solution.py:14
  542.3 11.3 %collective-permute-start = (bf16[256,512]{0,1:T(8,128)(2,1)S(1)}, bf16[256,512]{0,1:T(8,128)(2,1)S(1)}, u32[]{:S(2)}, u32[]{:S(2)}) collective-permute-start(bf16[256,512]{0,1:T(8,128)(2,1)S(1)} %get-tuple-element.781), channel_id=1, source_target_pairs={{0,4},{4,8},{8,12},{12,16},{16,20},{20,24},{24,28},{28,32},{32,36}... | collective-permute-start | bytes 786440 | tf_op jit(solution)/shard_map/while/body/eval_jaxpr/ppermute | solution.py:14
  563.6 11.3 %collective-permute-start = (bf16[256,512]{0,1:T(8,128)(2,1)S(1)}, bf16[256,512]{0,1:T(8,128)(2,1)S(1)}, u32[]{:S(2)}, u32[]{:S(2)}) collective-permute-start(bf16[256,512]{0,1:T(8,128)(2,1)S(1)} %get-tuple-element.781), channel_id=1, source_target_pairs={{0,4},{4,8},{8,12},{12,16},{16,20},{20,24},{24,28},{28,32},{32,36}... | collective-permute-start | bytes 786440 | tf_op jit(solution)/shard_map/while/body/eval_jaxpr/ppermute | solution.py:14
  584.8 11.3 %collective-permute-start = (bf16[256,512]{0,1:T(8,128)(2,1)S(1)}, bf16[256,512]{0,1:T(8,128)(2,1)S(1)}, u32[]{:S(2)}, u32[]{:S(2)}) collective-permute-start(bf16[256,512]{0,1:T(8,128)(2,1)S(1)} %get-tuple-element.781), channel_id=1, source_target_pairs={{0,4},{4,8},{8,12},{12,16},{16,20},{20,24},{24,28},{28,32},{32,36}... | collective-permute-start | bytes 786440 | tf_op jit(solution)/shard_map/while/body/eval_jaxpr/ppermute | solution.py:14
  606.1 11.3 %collective-permute-start = (bf16[256,512]{0,1:T(8,128)(2,1)S(1)}, bf16[256,512]{0,1:T(8,128)(2,1)S(1)}, u32[]{:S(2)}, u32[]{:S(2)}) collective-permute-start(bf16[256,512]{0,1:T(8,128)(2,1)S(1)} %get-tuple-element.781), channel_id=1, source_target_pairs={{0,4},{4,8},{8,12},{12,16},{16,20},{20,24},{24,28},{28,32},{32,36}... | collective-permute-start | bytes 786440 | tf_op jit(solution)/shard_map/while/body/eval_jaxpr/ppermute | solution.py:14
  627.3 11.3 %collective-permute-start = (bf16[256,512]{0,1:T(8,128)(2,1)S(1)}, bf16[256,512]{0,1:T(8,128)(2,1)S(1)}, u32[]{:S(2)}, u32[]{:S(2)}) collective-permute-start(bf16[256,512]{0,1:T(8,128)(2,1)S(1)} %get-tuple-element.781), channel_id=1, source_target_pairs={{0,4},{4,8},{8,12},{12,16},{16,20},{20,24},{24,28},{28,32},{32,36}... | collective-permute-start | bytes 786440 | tf_op jit(solution)/shard_map/while/body/eval_jaxpr/ppermute | solution.py:14
  648.6 11.3 %collective-permute-start = (bf16[256,512]{0,1:T(8,128)(2,1)S(1)}, bf16[256,512]{0,1:T(8,128)(2,1)S(1)}, u32[]{:S(2)}, u32[]{:S(2)}) collective-permute-start(bf16[256,512]{0,1:T(8,128)(2,1)S(1)} %get-tuple-element.781), channel_id=1, source_target_pairs={{0,4},{4,8},{8,12},{12,16},{16,20},{20,24},{24,28},{28,32},{32,36}... | collective-permute-start | bytes 786440 | tf_op jit(solution)/shard_map/while/body/eval_jaxpr/ppermute | solution.py:14
  669.8 11.3 %collective-permute-start = (bf16[256,512]{0,1:T(8,128)(2,1)S(1)}, bf16[256,512]{0,1:T(8,128)(2,1)S(1)}, u32[]{:S(2)}, u32[]{:S(2)}) collective-permute-start(bf16[256,512]{0,1:T(8,128)(2,1)S(1)} %get-tuple-element.781), channel_id=1, source_target_pairs={{0,4},{4,8},{8,12},{12,16},{16,20},{20,24},{24,28},{28,32},{32,36}... | collective-permute-start | bytes 786440 | tf_op jit(solution)/shard_map/while/body/eval_jaxpr/ppermute | solution.py:14
Sparse Core Ops, SparseCore 0:
  10.4 26.2 all-gather.2
where the time goes:
time: 700 us; the launch traced here: 695 us
  waiting for transfers between devices  227 us (32%)
  blocking collectives  172 us (25%)
  matrix products  106 us (15%)
  other arithmetic  62.5 us (9%)
  local copies, waits for them, and re-layouts  58.9 us (8%)
  starting transfers between devices  52.2 us (7%)
  between operations  14.1 us (2%)
    ppermute x21, waiting for transfers between devices, passed_along(): return lax.ppermute(shard, axis, pairs)  203 us
    all_gather x1, blocking collectives, on_device(): every_seg = lax.all_gather(segments, 'inst', axis=0, tiled=True)  172 us
    dot_general x21, matrix products, update(): jnp.einsum('oyce,eyk->oyck', weight_probs.astype(jnp.bfloat16), value_mat...  85 us
    ppermute x21, starting transfers between devices, passed_along(): return lax.ppermute(shard, axis, pairs)  41.1 us
    gather x21, local copies, waits for them, and re-layouts, update(): kseg = jnp.take(every_seg, jnp.clip(kpos, 0, total_rows - 1), axis=0)  36.2 us
    all_gather x1, waiting for transfers between devices, on_device(): source_rows = lax.all_gather(local_rows, 'head', axis=1, tiled=True)  23.7 us
    reduce_sum x21, other arithmetic, update(): total = total * factor + jnp.sum(weight_probs, axis=-1)  22.1 us
    dot_general x21, matrix products, update(): jnp.einsum('tgra,sga->tgrs', qgrid, kmat, preferred_element_type=jnp.floa...  18.2 us
  transfers between devices with their start and end apart: 23, of which 22 were waited for; matrix products, arithmetic and copies ran while one was open for 31% of the time, Pallas kernels for 0%

commit v1 on v0

v1 whole, which is shorter than its diff:
```python
import functools

import jax
import jax.numpy as jnp
from jax import lax
from jax.experimental import pallas as pl
from jax.experimental.pallas import tpu as pltpu
from jax.sharding import PartitionSpec as P

MESH = pl.DeviceIdType.MESH
F32, BF16 = jnp.float32, jnp.bfloat16

HEADS, SIZE, RATIO = 16, 128, 8
TOK = 256
REACH = 20
SLOT = 8
STEP = 4
SEG_ROW = 2 * TOK
BLOCK_ROWS = 2 * TOK + 16
TO_LOG2 = SIZE ** -0.5 * 1.4426950408889634

ARRIVALS = (
    ((16, 215, 109, 308, 301, 214, 307, 17, 102, 213, 306, 18, 212, 310, 211, 104, 305, 103, 20, 19),
     (16, 308, 215, 109, 214, 110, 101, 213, 307, 17, 102, 212, 103, 18, 111, 19, 306, 205, 204, 20)),
    ((16, 101, 308, 215, 117, 307, 110, 214, 302, 309, 213, 18, 212, 103, 19, 306, 211, 204, 305, 20),
     (101, 16, 215, 17, 308, 214, 309, 110, 213, 111, 102, 307, 18, 306, 205, 103, 104, 19, 212, 120)),
    ((101, 16, 308, 17, 215, 309, 102, 214, 18, 213, 111, 310, 212, 307, 303, 205, 306, 19, 304, 20),
     (16, 101, 215, 102, 308, 17, 214, 18, 307, 109, 310, 206, 111, 112, 213, 103, 119, 205, 104, 120)),
    ((101, 16, 17, 215, 308, 102, 214, 307, 18, 213, 103, 206, 309, 19, 310, 305, 212, 304, 111, 20),
     (16, 101, 215, 308, 17, 102, 214, 307, 103, 18, 309, 19, 110, 206, 111, 213, 112, 205, 104, 120)),
    ((101, 16, 215, 308, 17, 214, 207, 102, 213, 310, 18, 103, 206, 309, 19, 311, 204, 205, 20, 212),
     (16, 101, 215, 117, 308, 307, 102, 309, 18, 103, 214, 310, 19, 104, 206, 111, 20, 112, 113, 205)),
    ((16, 101, 215, 308, 102, 17, 307, 214, 18, 109, 205, 310, 103, 311, 19, 306, 104, 213, 112, 20),
     (101, 16, 308, 17, 215, 102, 309, 207, 18, 310, 103, 205, 19, 214, 104, 213, 20, 311, 206, 112)),
    ((16, 101, 308, 215, 206, 17, 102, 307, 103, 18, 310, 19, 214, 309, 213, 104, 311, 112, 20, 305),
     (101, 16, 17, 308, 102, 309, 206, 18, 215, 214, 103, 307, 110, 19, 104, 311, 205, 20, 213, 112)),
    ((16, 207, 101, 308, 17, 309, 102, 215, 18, 103, 214, 310, 104, 19, 111, 20, 213, 306, 105, 312),
     (101, 16, 207, 17, 308, 102, 215, 18, 309, 103, 310, 19, 220, 306, 214, 311, 104, 105, 312, 213)),
    ((308, 16, 215, 109, 317, 207, 101, 214, 102, 103, 18, 310, 19, 206, 213, 111, 205, 104, 320, 312),
     (16, 308, 215, 101, 207, 102, 17, 18, 309, 206, 214, 103, 310, 104, 19, 320, 311, 205, 213, 112)),
    ((16, 308, 101, 215, 109, 17, 110, 207, 318, 214, 102, 206, 103, 104, 19, 320, 213, 311, 205, 212),
     (101, 16, 308, 17, 309, 207, 215, 102, 214, 103, 18, 19, 310, 206, 212, 104, 313, 111, 20, 105)),
    ((16, 101, 308, 17, 309, 215, 102, 207, 110, 18, 214, 111, 319, 206, 103, 320, 212, 104, 213, 105),
     (308, 16, 101, 215, 102, 207, 17, 309, 18, 310, 206, 103, 213, 104, 314, 19, 20, 311, 205, 112)),
    ((101, 16, 308, 215, 17, 309, 102, 310, 18, 207, 206, 103, 311, 213, 112, 19, 314, 120, 205, 104),
     (16, 308, 101, 109, 215, 17, 207, 214, 102, 310, 103, 18, 311, 19, 206, 104, 205, 20, 213, 112)),
    ((16, 308, 101, 309, 207, 102, 17, 18, 214, 215, 103, 310, 19, 206, 311, 104, 113, 20, 312, 205),
     (101, 16, 308, 215, 17, 309, 207, 102, 110, 18, 206, 103, 311, 112, 19, 214, 204, 205, 120, 213)),
    ((308, 101, 16, 215, 17, 309, 207, 102, 310, 103, 18, 19, 214, 313, 104, 205, 311, 20, 112, 206),
     (16, 308, 101, 309, 207, 102, 17, 18, 215, 310, 205, 103, 111, 19, 206, 313, 104, 214, 312, 20)),
    ((16, 308, 101, 215, 102, 17, 309, 18, 314, 310, 206, 103, 207, 104, 19, 20, 213, 111, 105, 312),
     (308, 101, 16, 17, 309, 206, 207, 102, 215, 103, 18, 19, 314, 310, 213, 104, 311, 20, 312, 105)),
    ((16, 101, 207, 308, 17, 215, 309, 102, 103, 18, 310, 214, 19, 311, 104, 312, 105, 20, 213, 106),
     (207, 308, 16, 101, 309, 102, 17, 215, 18, 310, 214, 103, 311, 104, 19, 213, 20, 105, 312, 106)),
)


def offset_of(kind, link):
    y, z = divmod(kind, 8)
    return (16, 1 if z > 0 else -7, -1 if z < 7 else 7, 8 if y == 1 else -8)[link]


def target_of(kind, link):
    y, z = divmod(kind, 8)
    return (kind, y * 8 + (z + 1) % 8, y * 8 + (z + 7) % 8, (1 - y) * 8 + z)[link]


def forward_table():
    table = []
    for kind in range(16):
        halves = []
        for half in range(2):
            held = [0] + [a % 100 for a in ARRIVALS[kind][half]]
            rows = []
            for distance in held:
                row = []
                for link in range(4):
                    there = target_of(kind, link)
                    far = distance + offset_of(there, link)
                    order = ARRIVALS[there][half]
                    wanted = link * 100 + far
                    row.append(order.index(wanted) + 1 if 1 <= far <= REACH and wanted in order else 0)
                rows.append(row)
            halves.append(rows)
        table.append(halves)
    return table


TABLE = forward_table()


def kernel(q_hbm, k_hbm, v_hbm, seg_hbm, own_hbm, out_ref, cache_ref,
           q_ref, seg_ref, own_ref, kv, bias, top, total, acc, outgoing, mid, recv, block,
           in_sem, kv_send, kv_recv, z_send, z_recv, x_send, x_recv, y_send, y_recv, c_send, c_recv, own_sem):
    me, g = lax.axis_index("inst"), lax.axis_index("head")
    kind = me % 16
    x, y, z = me // 16, (me // 8) % 2, me % 8
    other_y = x * 16 + (1 - y) * 8 + z
    other_chip, other_core = (g + 2) % 4, g + 1 - 2 * (g % 2)
    near = (
        ((x + 1) % 4) * 16 + kind,
        me - z + (z + 1) % 8,
        me - z + (z + 7) % 8,
        other_y,
    )

    inputs = [
        pltpu.make_async_copy(k_hbm.at[:, half * SIZE:(half + 1) * SIZE], kv.at[half, 0, 0:TOK], in_sem.at[half])
        for half in range(2)
    ] + [
        pltpu.make_async_copy(v_hbm.at[:, half * SIZE:(half + 1) * SIZE], kv.at[half, 0, TOK:2 * TOK], in_sem.at[2 + half])
        for half in range(2)
    ] + [
        pltpu.make_async_copy(seg_hbm, seg_ref, in_sem.at[4]),
        pltpu.make_async_copy(own_hbm, own_ref, in_sem.at[5]),
        pltpu.make_async_copy(q_hbm, q_ref, in_sem.at[6]),
    ]
    for copy in inputs:
        copy.start()

    def along_z(by):
        return (me - z + (z + by) % 8, g)

    def along_x(by):
        return (((x + by) % 4) * 16 + kind, g)

    beside = ((me, other_chip), (other_y, g), (other_y, other_chip))
    sibling = (me, other_core)
    barrier = pltpu.get_barrier_semaphore()
    partners = [along_z(by) for by in range(1, 8)] + [along_x(by) for by in range(1, 4)] + list(beside) + [sibling]
    for partner in partners:
        pl.semaphore_signal(barrier, inc=1, device_id=partner, device_id_type=MESH)

    def pick(values):
        chosen = jnp.int32(values[0])
        if len(set(values)) == 1:
            return chosen
        for t in range(1, 16):
            chosen = jnp.where(kind == t, jnp.int32(values[t]), chosen)
        return chosen

    first = [[pick([TABLE[t][half][0][link] for t in range(16)]) for link in range(4)] for half in range(2)]
    codes = [
        [
            [pick([sum(TABLE[t][half][STEP * k + jj + 1][link] * 64 ** k for k in range(5)) for t in range(16)]) for link in range(4)]
            for jj in range(STEP)
        ]
        for half in range(2)
    ]

    def digits(half, jj, k):
        return [(codes[half][jj][link] >> (6 * k)) & 63 for link in range(4)]

    def forward(half, slot, theres, wait=False):
        for link in range(4):
            there = theres[link]

            @pl.when(there > 0)
            def _():
                copy = pltpu.make_async_remote_copy(
                    src_ref=kv.at[half, slot],
                    dst_ref=kv.at[half, there],
                    send_sem=kv_send.at[half * 4 + link, slot],
                    recv_sem=kv_recv.at[half, there],
                    device_id=(near[link], g),
                    device_id_type=MESH,
                )
                if wait:
                    copy.wait_send()
                else:
                    copy.start()

    def arrive(k, h, j):
        half, jj = j % 2, 2 * h + j // 2
        slot = STEP * k + jj + 1
        pltpu.make_async_copy(kv.at[half, slot], kv.at[half, slot], kv_recv.at[half, slot]).wait()
        forward(half, slot, digits(half, jj, k))

    for copy in inputs[:5]:
        copy.wait()
    seg_row = seg_ref[...].astype(F32)
    seg_wide = jnp.broadcast_to(seg_row, (TOK, TOK))
    for half in range(2):
        kv[half, 0, SEG_ROW:BLOCK_ROWS, :] = jnp.concatenate(
            [jnp.broadcast_to(seg_row[:, 0:SIZE], (8, SIZE)), jnp.broadcast_to(seg_row[:, SIZE:], (8, SIZE))], axis=0
        ).astype(BF16)
    pl.semaphore_wait(barrier, len(partners))
    forward(0, 0, first[0])
    forward(1, 0, first[1])

    inputs[5].wait()
    dest = own_ref[...]
    owner = lax.broadcasted_iota(jnp.int32, (64, TOK), 0)
    hot = (owner == dest).astype(F32)
    before = (lax.broadcasted_iota(jnp.int32, (TOK, TOK), 0) < lax.broadcasted_iota(jnp.int32, (TOK, TOK), 1)).astype(BF16)
    count = jnp.dot(hot.astype(BF16), before, preferred_element_type=F32)
    place = jnp.sum(hot * count, axis=0, keepdims=True).astype(jnp.int32)
    target = dest * (2 * SLOT) + place
    row = lax.broadcasted_iota(jnp.int32, (1024, TOK), 0)
    of_keys = (row == target).astype(BF16)
    of_values = (row == target + SLOT).astype(BF16)
    for half in range(2):
        rows = jnp.dot(of_keys, kv[half, 0, 0:TOK, :], preferred_element_type=F32)
        rows += jnp.dot(of_values, kv[half, 0, TOK:2 * TOK, :], preferred_element_type=F32)
        outgoing[:, :, :, :, half * SIZE:(half + 1) * SIZE] = rows.astype(BF16).reshape(4, 2, 8, 2 * SLOT, SIZE)

    def z_copy(by):
        return pltpu.make_async_remote_copy(
            src_ref=outgoing.at[:, :, (z + by) % 8], dst_ref=mid.at[z], send_sem=z_send.at[by], recv_sem=z_recv.at[z],
            device_id=along_z(by), device_id_type=MESH)

    def x_copy(by):
        return pltpu.make_async_remote_copy(
            src_ref=mid.at[:, (x + by) % 4], dst_ref=recv.at[x], send_sem=x_send.at[by], recv_sem=x_recv.at[x],
            device_id=along_x(by), device_id_type=MESH)

    def rows_of(source_y, group):
        return cache_ref.at[:, source_y, :, pl.ds(pl.multiple_of(group * 512, 512), 512)]

    def y_copy(n):
        return pltpu.make_async_remote_copy(
            src_ref=block.at[y if n == 0 else 1 - y], dst_ref=rows_of(y, g), send_sem=y_send.at[n], recv_sem=y_recv.at[n],
            device_id=beside[n], device_id_type=MESH)

    from_y = ((y, other_chip), (1 - y, g), (1 - y, other_chip))

    def c_copy(n):
        if n == 3:
            src, place = block.at[y], rows_of(y, g)
        else:
            src = place = rows_of(*from_y[n])
        return pltpu.make_async_remote_copy(
            src_ref=src, dst_ref=place, send_sem=c_send.at[n], recv_sem=c_recv.at[n],
            device_id=sibling, device_id_type=MESH)

    def own_copy():
        return pltpu.make_async_copy(block.at[y], rows_of(y, g), own_sem)

    def first_leg():
        for by in (1, 7, 2, 6, 3, 5, 4):
            z_copy(by).start()
        for i in range(4):
            for j in range(2):
                mid[z, i, j] = outgoing[i, j, z]

    def second_leg():
        for by in range(1, 8):
            src = (z + 8 - by) % 8
            pltpu.make_async_copy(mid.at[src], mid.at[src], z_recv.at[src]).wait()
        for by in (1, 3, 2):
            x_copy(by).start()
        for i in range(8):
            recv[x, i] = mid[i, x]

    def third_leg():
        for by in range(1, 4):
            src = (x + 4 - by) % 4
            pltpu.make_async_copy(recv.at[src], recv.at[src], x_recv.at[src]).wait()
        a = lax.broadcasted_iota(jnp.int32, (64, 128), 0)
        b = lax.broadcasted_iota(jnp.int32, (64, 128), 1)
        key_rows = (b == 2 * a - (a & 7)).astype(BF16)
        value_rows = (b == 2 * a - (a & 7) + 8).astype(BF16)
        for src in range(4):
            for j in range(2):
                arrived = recv[src, :, j].reshape(128, 2 * SIZE)
                block[j, src, :, 0:256] = jnp.dot(key_rows, arrived, preferred_element_type=F32).astype(BF16)
                block[j, src, :, 256:512] = jnp.dot(value_rows, arrived, preferred_element_type=F32).astype(BF16)
        for n in range(3):
            y_copy(n).start()
        c_copy(3).start()
        own_copy().start()

    def fourth_leg():
        for n in range(3):
            here = rows_of(*from_y[n])
            pltpu.make_async_copy(here, here, y_recv.at[n]).wait()
            c_copy(n).start()

    at0 = lax.broadcasted_iota(jnp.int32, (TOK, TOK), 0)
    at1 = lax.broadcasted_iota(jnp.int32, (TOK, TOK), 1)
    seg_col = jnp.sum(jnp.where(at0 == at1, seg_wide, 0.0), axis=1, keepdims=True)
    seg_col = jnp.broadcast_to(seg_col, (TOK, SIZE))
    seg_both = jnp.concatenate([seg_col, seg_col], axis=1)
    bias[:, 0:TOK] = jnp.where((seg_both == seg_wide) & (at0 >= at1), 0.0, -1e30)

    def head_scores(h, slot, c):
        q_h = q_ref[:, h * SIZE:(h + 1) * SIZE]
        scores = lax.dot_general(q_h, kv[h // RATIO, slot, 0:TOK, :], (((1,), (1,)), ((), ())), preferred_element_type=F32)
        return scores + bias[:, c * TOK:(c + 1) * TOK]

    def weighted(h, slot, scores, peak):
        weights = jnp.exp2((scores - jnp.concatenate([peak, peak], axis=1)) * TO_LOG2)
        product = jnp.dot(weights.astype(BF16), kv[h // RATIO, slot, TOK:2 * TOK, :], preferred_element_type=F32)
        return weights[:, 0:SIZE] + weights[:, SIZE:], product

    inputs[6].wait()
    for half in range(2):
        for j in range(4):
            for h in range(half * RATIO + 2 * j, half * RATIO + 2 * j + 2):
                scores = head_scores(h, 0, 0)
                peak = jnp.broadcast_to(jnp.max(scores, axis=1, keepdims=True), (TOK, SIZE))
                part, product = weighted(h, 0, scores, peak)
                top[h], total[h], acc[h] = peak, part, product
            arrive(0, half, j)
        if half == 0:
            first_leg()
    second_leg()

    def step(k, carry):
        for half in range(2):
            slots = [STEP * k + 1 + c for c in range(STEP)]
            for c in range(STEP):
                seg_rows = kv[half, slots[c], SEG_ROW:BLOCK_ROWS, :].astype(F32)
                for part in range(2):
                    key_seg = jnp.broadcast_to(seg_rows[8 * part:8 * part + 1, :], (TOK, SIZE))
                    at = c * TOK + part * SIZE
                    bias[:, at:at + SIZE] = jnp.where(seg_col == key_seg, 0.0, -1e30)
            for j in range(4):
                for h in range(half * RATIO + 2 * j, half * RATIO + 2 * j + 2):
                    scores = [head_scores(h, slots[c], c) for c in range(STEP)]
                    largest = functools.reduce(jnp.maximum, scores)
                    old = top[h]
                    peak = jnp.maximum(old, jnp.max(largest, axis=1, keepdims=True))
                    shrink = jnp.exp2((old - peak) * TO_LOG2)
                    parts, products = zip(*[weighted(h, slots[c], scores[c], peak) for c in range(STEP)])
                    top[h] = peak
                    total[h] = total[h] * shrink + sum(parts[1:], parts[0])
                    acc[h] = acc[h] * shrink + sum(products[1:], products[0])

                @pl.when(k < 4)
                def _():
                    arrive(k + 1, half, j)

        @pl.when(k == 1)
        def _():
            third_leg()

        @pl.when(k == 3)
        def _():
            fourth_leg()

        return carry

    lax.fori_loop(0, 5, step, 0)

    for h in range(HEADS):
        denominator = jnp.sum(total[h], axis=1, keepdims=True)
        out_ref[:, h * SIZE:(h + 1) * SIZE] = (acc[h] / denominator).astype(BF16)

    for half in range(2):
        forward(half, 0, first[half], wait=True)

    def drain(k, carry):
        for half in range(2):
            for jj in range(STEP):
                forward(half, STEP * k + jj + 1, digits(half, jj, k), wait=True)
        return carry

    lax.fori_loop(0, 5, drain, 0)
    for by in range(1, 8):
        z_copy(by).wait_send()
    for by in range(1, 4):
        x_copy(by).wait_send()
    for n in range(3):
        y_copy(n).wait_send()
    own_copy().wait()
    across = (other_core + 2) % 4
    from_core = ((y, across), (1 - y, other_core), (1 - y, across), (y, other_core))
    for n in range(4):
        c_copy(n).wait_send()
        here = rows_of(*from_core[n])
        pltpu.make_async_copy(here, here, c_recv.at[n]).wait()


def on_device(queries, keys, values, segments, owners):
    whole = pl.BlockSpec(memory_space=pl.ANY)
    attended, cache = pl.pallas_call(
        kernel,
        out_shape=(
            jax.ShapeDtypeStruct((TOK, HEADS * SIZE), BF16),
            jax.ShapeDtypeStruct((4, 2, 64, 2048), BF16),
        ),
        in_specs=[whole] * 5,
        out_specs=(pl.BlockSpec(memory_space=pltpu.VMEM), whole),
        scratch_shapes=[
            pltpu.VMEM((TOK, HEADS * SIZE), BF16),
            pltpu.VMEM((1, TOK), jnp.int32),
            pltpu.VMEM((1, TOK), jnp.int32),
            pltpu.VMEM((2, REACH + 1, BLOCK_ROWS, SIZE), BF16),
            pltpu.VMEM((TOK, STEP * TOK), F32),
            pltpu.VMEM((HEADS, TOK, SIZE), F32),
            pltpu.VMEM((HEADS, TOK, SIZE), F32),
            pltpu.VMEM((HEADS, TOK, SIZE), F32),
            pltpu.VMEM((4, 2, 8, 2 * SLOT, 2 * SIZE), BF16),
            pltpu.VMEM((8, 4, 2, 2 * SLOT, 2 * SIZE), BF16),
            pltpu.VMEM((4, 8, 2, 2 * SLOT, 2 * SIZE), BF16),
            pltpu.VMEM((2, 4, 64, 4 * SIZE), BF16),
            pltpu.SemaphoreType.DMA((7,)),
            pltpu.SemaphoreType.DMA((8, REACH + 1)),
            pltpu.SemaphoreType.DMA((2, REACH + 1)),
            pltpu.SemaphoreType.DMA((8,)),
            pltpu.SemaphoreType.DMA((8,)),
            pltpu.SemaphoreType.DMA((4,)),
            pltpu.SemaphoreType.DMA((4,)),
            pltpu.SemaphoreType.DMA((3,)),
            pltpu.SemaphoreType.DMA((3,)),
            pltpu.SemaphoreType.DMA((4,)),
            pltpu.SemaphoreType.DMA((4,)),
            pltpu.SemaphoreType.DMA(()),
        ],
        compiler_params=pltpu.CompilerParams(
            collective_id=0, has_side_effects=True, vmem_limit_bytes=56 * 1024 * 1024
        ),
        cost_estimate=pl.CostEstimate(flops=12_000_000_000, bytes_accessed=6_000_000, transcendentals=22_000_000),
        name="attend_and_send",
    )(queries, keys, values, segments.reshape(1, TOK), owners.reshape(1, TOK))
    return attended, cache.reshape(64 * SLOT, 2048)


def solution(mesh):
    return jax.shard_map(
        on_device,
        mesh=mesh,
        in_specs=(
            P("inst", "head"),
            P("inst", "head"),
            P("inst", "head"),
            P("inst"),
            P("inst", None),
        ),
        out_specs=(P("inst", "head"), P("inst", None)),
        check_vma=False,
    )
```

time: 700 us -> 110 us (0.16)
  the two profiles are of different devices: /device:TPU:6 before, /device:TPU:2 now
where the time goes in v1:
time: 110 us
  Pallas kernels  105 us (95%)
  local copies, waits for them, and re-layouts  3.78 us (3%)
    pallas_call x1, Pallas kernels, on_device(): pl.pallas_call(kernel, out_shape=(jax.ShapeDtypeStruct((TOK, HEADS * SIZE...  105 us
    unnamed x4, local copies, waits for them, and re-layouts  3.78 us

profile of v1, /device:TPU:2, one launch (start us, length us, event | category | flops | bytes accessed | tf_op | source)
XLA Modules:
  0.0 109.6 jit_solution(1220142910694818060)
XLA Ops:
  0.6 105.2 %attend_and_send.1 = (bf16[256,2048]{1,0:T(8,128)(2,1)}, bf16[4,2,64,2048]{3,2,1,0:T(8,128)(2,1)}) custom-call(bf16[256,2048]{1,0:T(8,128)(2,1)} %q_hbm.1, bf16[256,256]{1,0:T(8,128)(2,1)} %k_hbm.1, bf16[256,256]{1,0:T(8,128)(2,1)} %v_hbm.1, s32[1,256]{1,0:T(1,128)} %bitcast.4, s32[1,256]{1,0:T(1,128)} %bitcast.5), custom_call_target="tpu_custom_call" | custom-call | flops 12000000000 | bytes 6000000 | tf_op jit(solution)/shard_map/attend_and_send/pallas_call | solution.py:377
  105.8 0.0 copy-start
  105.9 2.5 %copy.9 = bf16[256,2048]{1,0:T(8,128)(2,1)} copy(bf16[256,2048]{1,0:T(8,128)(2,1)} %get-tuple-element.8) | data formatting | bytes 2097152
  108.3 0.0 copy-done
  108.3 1.3 %copy.10 = bf16[512,2048]{1,0:T(8,128)(2,1)} copy(bf16[512,2048]{1,0:T(8,128)(2,1)S(1)} %bitcast.3) | data formatting | bytes 4194304
Async XLA Ops:
  105.8 2.5 %copy-start = (bf16[4,2,64,2048]{3,2,1,0:T(8,128)(2,1)S(1)}, bf16[4,2,64,2048]{3,2,1,0:T(8,128)(2,1)}, u32[]{:S(2)}) copy-start(bf16[4,2,64,2048]{3,2,1,0:T(8,128)(2,1)} %get-tuple-element.5) | copy-start | bytes 6291460

commit v2 on v1

--- a/solution.py
+++ b/solution.py
@@ -15,8 +15,9 @@
 REACH = 20
 SLOT = 8
 STEP = 4
-SEG_ROW = 2 * TOK
-BLOCK_ROWS = 2 * TOK + 16
+KEY_ROW, MASK_ROW, SENT_ROWS, ALL_ROWS = 128, 256, 272, 384
+FAR = 1024.0
+ROWS = 16
 TO_LOG2 = SIZE ** -0.5 * 1.4426950408889634
 
 ARRIVALS = (
@@ -90,8 +91,9 @@
 
 
 def kernel(q_hbm, k_hbm, v_hbm, seg_hbm, own_hbm, out_ref, cache_ref,
-           q_ref, seg_ref, own_ref, kv, bias, top, total, acc, outgoing, mid, recv, block,
-           in_sem, kv_send, kv_recv, z_send, z_recv, x_send, x_recv, y_send, y_recv, c_send, c_recv, own_sem):
+           q_aug, k_own, v_own, seg_ref, own_ref, kv, bias, top, total, acc, scores_a, scores_b, weights_a, weights_b, shrink_a, shrink_b,
+           outgoing, mid, recv, block,
+           in_sem, q_sem, kv_send, kv_recv, z_send, z_recv, x_send, x_recv, y_send, y_recv, c_send, c_recv, own_sem):
     me, g = lax.axis_index("inst"), lax.axis_index("head")
     kind = me % 16
     x, y, z = me // 16, (me // 8) % 2, me % 8
@@ -105,17 +107,13 @@
     )
 
     inputs = [
-        pltpu.make_async_copy(k_hbm.at[:, half * SIZE:(half + 1) * SIZE], kv.at[half, 0, 0:TOK], in_sem.at[half])
-        for half in range(2)
-    ] + [
-        pltpu.make_async_copy(v_hbm.at[:, half * SIZE:(half + 1) * SIZE], kv.at[half, 0, TOK:2 * TOK], in_sem.at[2 + half])
-        for half in range(2)
-    ] + [
-        pltpu.make_async_copy(seg_hbm, seg_ref, in_sem.at[4]),
-        pltpu.make_async_copy(own_hbm, own_ref, in_sem.at[5]),
-        pltpu.make_async_copy(q_hbm, q_ref, in_sem.at[6]),
+        pltpu.make_async_copy(src, dst, in_sem.at[n])
+        for n, (src, dst) in enumerate(((k_hbm, k_own), (v_hbm, v_own), (seg_hbm, seg_ref), (own_hbm, own_ref)))
     ]
-    for copy in inputs:
+    queries = [
+        pltpu.make_async_copy(q_hbm.at[:, h * SIZE:(h + 1) * SIZE], q_aug.at[h, :, 0:SIZE], q_sem.at[h]) for h in range(HEADS)
+    ]
+    for copy in inputs + queries:
         copy.start()
 
     def along_z(by):
@@ -158,8 +156,8 @@
             @pl.when(there > 0)
             def _():
                 copy = pltpu.make_async_remote_copy(
-                    src_ref=kv.at[half, slot],
-                    dst_ref=kv.at[half, there],
+                    src_ref=kv.at[half, slot, 0:SENT_ROWS],
+                    dst_ref=kv.at[half, there, 0:SENT_ROWS],
                     send_sem=kv_send.at[half * 4 + link, slot],
                     recv_sem=kv_recv.at[half, there],
                     device_id=(near[link], g),
@@ -173,22 +171,33 @@
     def arrive(k, h, j):
         half, jj = j % 2, 2 * h + j // 2
         slot = STEP * k + jj + 1
-        pltpu.make_async_copy(kv.at[half, slot], kv.at[half, slot], kv_recv.at[half, slot]).wait()
+        here = kv.at[half, slot, 0:SENT_ROWS]
+        pltpu.make_async_copy(here, here, kv_recv.at[half, slot]).wait()
         forward(half, slot, digits(half, jj, k))
 
-    for copy in inputs[:5]:
+    for copy in inputs[:3]:
         copy.wait()
     seg_row = seg_ref[...].astype(F32)
     seg_wide = jnp.broadcast_to(seg_row, (TOK, TOK))
+    request = lax.broadcasted_iota(jnp.int32, (16, TOK), 0).astype(F32)
     for half in range(2):
-        kv[half, 0, SEG_ROW:BLOCK_ROWS, :] = jnp.concatenate(
-            [jnp.broadcast_to(seg_row[:, 0:SIZE], (8, SIZE)), jnp.broadcast_to(seg_row[:, SIZE:], (8, SIZE))], axis=0
-        ).astype(BF16)
+        feat = slice(half * SIZE, (half + 1) * SIZE)
+        kv[half, 0, 0:KEY_ROW, 0:SIZE] = v_own[0:SIZE, feat]
+        kv[half, 0, 0:KEY_ROW, SIZE:TOK] = v_own[SIZE:TOK, feat]
+        kv[half, 0, KEY_ROW:MASK_ROW, :] = k_own[:, feat].astype(F32).T.astype(BF16)
+        kv[half, 0, MASK_ROW:SENT_ROWS, :] = jnp.where(seg_wide[0:16] == request, 0.0, -FAR).astype(BF16)
     pl.semaphore_wait(barrier, len(partners))
     forward(0, 0, first[0])
     forward(1, 0, first[1])
 
-    inputs[5].wait()
+    def clear(slot, carry):
+        for half in range(2):
+            kv[half, slot, SENT_ROWS:ALL_ROWS, :] = jnp.zeros((ALL_ROWS - SENT_ROWS, TOK), BF16)
+        return carry
+
+    lax.fori_loop(0, REACH + 1, clear, 0)
+
+    inputs[3].wait()
     dest = own_ref[...]
     owner = lax.broadcasted_iota(jnp.int32, (64, TOK), 0)
     hot = (owner == dest).astype(F32)
@@ -199,10 +208,9 @@
     row = lax.broadcasted_iota(jnp.int32, (1024, TOK), 0)
     of_keys = (row == target).astype(BF16)
     of_values = (row == target + SLOT).astype(BF16)
-    for half in range(2):
-        rows = jnp.dot(of_keys, kv[half, 0, 0:TOK, :], preferred_element_type=F32)
-        rows += jnp.dot(of_values, kv[half, 0, TOK:2 * TOK, :], preferred_element_type=F32)
-        outgoing[:, :, :, :, half * SIZE:(half + 1) * SIZE] = rows.astype(BF16).reshape(4, 2, 8, 2 * SLOT, SIZE)
+    rows = jnp.dot(of_keys, k_own[...], preferred_element_type=F32)
+    rows += jnp.dot(of_values, v_own[...], preferred_element_type=F32)
+    outgoing[...] = rows.astype(BF16).reshape(4, 2, 8, 2 * SLOT, 2 * SIZE)
 
     def z_copy(by):
         return pltpu.make_async_remote_copy(
@@ -279,28 +287,64 @@
     at0 = lax.broadcasted_iota(jnp.int32, (TOK, TOK), 0)
     at1 = lax.broadcasted_iota(jnp.int32, (TOK, TOK), 1)
     seg_col = jnp.sum(jnp.where(at0 == at1, seg_wide, 0.0), axis=1, keepdims=True)
-    seg_col = jnp.broadcast_to(seg_col, (TOK, SIZE))
-    seg_both = jnp.concatenate([seg_col, seg_col], axis=1)
-    bias[:, 0:TOK] = jnp.where((seg_both == seg_wide) & (at0 >= at1), 0.0, -1e30)
-
-    def head_scores(h, slot, c):
-        q_h = q_ref[:, h * SIZE:(h + 1) * SIZE]
-        scores = lax.dot_general(q_h, kv[h // RATIO, slot, 0:TOK, :], (((1,), (1,)), ((), ())), preferred_element_type=F32)
-        return scores + bias[:, c * TOK:(c + 1) * TOK]
-
-    def weighted(h, slot, scores, peak):
-        weights = jnp.exp2((scores - jnp.concatenate([peak, peak], axis=1)) * TO_LOG2)
-        product = jnp.dot(weights.astype(BF16), kv[h // RATIO, slot, TOK:2 * TOK, :], preferred_element_type=F32)
-        return weights[:, 0:SIZE] + weights[:, SIZE:], product
-
-    inputs[6].wait()
+    lane = lax.broadcasted_iota(jnp.int32, (TOK, SIZE), 1).astype(F32)
+    query_mask = jnp.where(lane == seg_col, FAR, 0.0).astype(BF16)
+    for h in range(HEADS):
+        q_aug[h, :, SIZE:2 * SIZE] = query_mask
+    bias[...] = jnp.where(at0 >= at1, 0.0, -1e30)
+    scores_of, weights_of, shrink_of = (scores_a, scores_b), (weights_a, weights_b), (shrink_a, shrink_b)
+
+    def unit(half, slots, diagonal):
+        width = len(slots) * TOK
+
+        def score(i, c):
+            scores_of[i % 2][:, c * TOK:(c + 1) * TOK] = jnp.dot(
+                q_aug[half * RATIO + i], kv[half, slots[c], KEY_ROW:ALL_ROWS, :], preferred_element_type=F32)
+
+        def soften(i, at):
+            h, rows = half * RATIO + i, slice(at, at + ROWS)
+            parts = [scores_of[i % 2][rows, j:j + SIZE] for j in range(0, width, SIZE)]
+            if diagonal:
+                parts = [part + bias[rows, n * SIZE:(n + 1) * SIZE] for n, part in enumerate(parts)]
+            largest = jnp.max(functools.reduce(jnp.maximum, parts), axis=1, keepdims=True)
+            if diagonal:
+                peak = jnp.broadcast_to(largest, (ROWS, SIZE))
+            else:
+                old = top[h, rows, :]
+                peak = jnp.maximum(old, largest)
+                shrink = jnp.exp2((old - peak) * TO_LOG2)
+                shrink_of[i % 2][rows, :] = shrink
+            weights = [jnp.exp2((part - peak) * TO_LOG2) for part in parts]
+            for n, weight in enumerate(weights):
+                weights_of[i % 2][rows, n * SIZE:(n + 1) * SIZE] = weight.astype(BF16)
+            added = functools.reduce(jnp.add, weights)
+            top[h, rows, :] = peak
+            total[h, rows, :] = added if diagonal else total[h, rows, :] * shrink + added
+
+        def combine(i):
+            h = half * RATIO + i
+            values = jnp.concatenate(
+                [kv[half, slot, 0:KEY_ROW, lanes:lanes + SIZE] for slot in slots for lanes in (0, SIZE)], axis=0)
+            product = jnp.dot(weights_of[i % 2][:, 0:width], values, preferred_element_type=F32)
+            acc[h] = product if diagonal else acc[h] * shrink_of[i % 2][...] + product
+
+        for c in range(len(slots)):
+            score(0, c)
+        for i in range(RATIO):
+            for quarter in range(4):
+                if i + 1 < RATIO and quarter < len(slots):
+                    score(i + 1, quarter)
+                for at in range(quarter * 64, quarter * 64 + 64, ROWS):
+                    soften(i, at)
+                if quarter == 1 and i > 0:
+                    combine(i - 1)
+        combine(RATIO - 1)
+
+    for copy in queries:
+        copy.wait()
     for half in range(2):
+        unit(half, [0], True)
         for j in range(4):
-            for h in range(half * RATIO + 2 * j, half * RATIO + 2 * j + 2):
-                scores = head_scores(h, 0, 0)
-                peak = jnp.broadcast_to(jnp.max(scores, axis=1, keepdims=True), (TOK, SIZE))
-                part, product = weighted(h, 0, scores, peak)
-                top[h], total[h], acc[h] = peak, part, product
             arrive(0, half, j)
         if half == 0:
             first_leg()
@@ -308,27 +352,11 @@
 
     def step(k, carry):
         for half in range(2):
-            slots = [STEP * k + 1 + c for c in range(STEP)]
-            for c in range(STEP):
-                seg_rows = kv[half, slots[c], SEG_ROW:BLOCK_ROWS, :].astype(F32)
-                for part in range(2):
-                    key_seg = jnp.broadcast_to(seg_rows[8 * part:8 * part + 1, :], (TOK, SIZE))
-                    at = c * TOK + part * SIZE
-                    bias[:, at:at + SIZE] = jnp.where(seg_col == key_seg, 0.0, -1e30)
-            for j in range(4):
-                for h in range(half * RATIO + 2 * j, half * RATIO + 2 * j + 2):
-                    scores = [head_scores(h, slots[c], c) for c in range(STEP)]
-                    largest = functools.reduce(jnp.maximum, scores)
-                    old = top[h]
-                    peak = jnp.maximum(old, jnp.max(largest, axis=1, keepdims=True))
-                    shrink = jnp.exp2((old - peak) * TO_LOG2)
-                    parts, products = zip(*[weighted(h, slots[c], scores[c], peak) for c in range(STEP)])
-                    top[h] = peak
-                    total[h] = total[h] * shrink + sum(parts[1:], parts[0])
-                    acc[h] = acc[h] * shrink + sum(products[1:], products[0])
-
-                @pl.when(k < 4)
-                def _():
+            unit(half, [STEP * k + 1 + c for c in range(STEP)], False)
+
+            @pl.when(k < 4)
+            def _():
+                for j in range(4):
                     arrive(k + 1, half, j)
 
         @pl.when(k == 1)
@@ -383,19 +411,28 @@
         in_specs=[whole] * 5,
         out_specs=(pl.BlockSpec(memory_space=pltpu.VMEM), whole),
         scratch_shapes=[
-            pltpu.VMEM((TOK, HEADS * SIZE), BF16),
+            pltpu.VMEM((HEADS, TOK, 2 * SIZE), BF16),
+            pltpu.VMEM((TOK, 2 * SIZE), BF16),
+            pltpu.VMEM((TOK, 2 * SIZE), BF16),
             pltpu.VMEM((1, TOK), jnp.int32),
             pltpu.VMEM((1, TOK), jnp.int32),
-            pltpu.VMEM((2, REACH + 1, BLOCK_ROWS, SIZE), BF16),
-            pltpu.VMEM((TOK, STEP * TOK), F32),
+            pltpu.VMEM((2, REACH + 1, ALL_ROWS, TOK), BF16),
+            pltpu.VMEM((TOK, TOK), F32),
             pltpu.VMEM((HEADS, TOK, SIZE), F32),
             pltpu.VMEM((HEADS, TOK, SIZE), F32),
             pltpu.VMEM((HEADS, TOK, SIZE), F32),
+            pltpu.VMEM((TOK, STEP * TOK), F32),
+            pltpu.VMEM((TOK, STEP * TOK), F32),
+            pltpu.VMEM((TOK, STEP * TOK), BF16),
+            pltpu.VMEM((TOK, STEP * TOK), BF16),
+            pltpu.VMEM((TOK, SIZE), F32),
+            pltpu.VMEM((TOK, SIZE), F32),
             pltpu.VMEM((4, 2, 8, 2 * SLOT, 2 * SIZE), BF16),
             pltpu.VMEM((8, 4, 2, 2 * SLOT, 2 * SIZE), BF16),
             pltpu.VMEM((4, 8, 2, 2 * SLOT, 2 * SIZE), BF16),
             pltpu.VMEM((2, 4, 64, 4 * SIZE), BF16),
-            pltpu.SemaphoreType.DMA((7,)),
+            pltpu.SemaphoreType.DMA((4,)),
+            pltpu.SemaphoreType.DMA((HEADS,)),
             pltpu.SemaphoreType.DMA((8, REACH + 1)),
             pltpu.SemaphoreType.DMA((2, REACH + 1)),
             pltpu.SemaphoreType.DMA((8,)),

time: 110 us -> 105 us (0.955)
  the two profiles are of different devices: /device:TPU:2 before, /device:TPU:18 now
where the time goes in v2:
time: 105 us
  Pallas kernels  101 us (96%)
  local copies, waits for them, and re-layouts  3.78 us (4%)
    pallas_call x1, Pallas kernels, on_device(): pl.pallas_call(kernel, out_shape=(jax.ShapeDtypeStruct((TOK, HEADS * SIZE...  101 us
    unnamed x4, local copies, waits for them, and re-layouts  3.78 us

profile of v2, /device:TPU:18, one launch (start us, length us, event | category | flops | bytes accessed | tf_op | source)
XLA Modules:
  0.0 105.0 jit_solution(18414926887191615012)
XLA Ops:
  0.6 100.5 %attend_and_send.1 = (bf16[256,2048]{1,0:T(8,128)(2,1)}, bf16[4,2,64,2048]{3,2,1,0:T(8,128)(2,1)}) custom-call(bf16[256,2048]{1,0:T(8,128)(2,1)} %q_hbm.1, bf16[256,256]{1,0:T(8,128)(2,1)} %k_hbm.1, bf16[256,256]{1,0:T(8,128)(2,1)} %v_hbm.1, s32[1,256]{1,0:T(1,128)} %bitcast.4, s32[1,256]{1,0:T(1,128)} %bitcast.5), custom_call_target="tpu_custom_call" | custom-call | flops 12000000000 | bytes 6000000 | tf_op jit(solution)/shard_map/attend_and_send/pallas_call | solution.py:405
  101.2 0.0 copy-start
  101.2 2.5 %copy.9 = bf16[256,2048]{1,0:T(8,128)(2,1)} copy(bf16[256,2048]{1,0:T(8,128)(2,1)} %get-tuple-element.8) | data formatting | bytes 2097152
  103.6 0.0 copy-done
  103.6 1.3 %copy.10 = bf16[512,2048]{1,0:T(8,128)(2,1)} copy(bf16[512,2048]{1,0:T(8,128)(2,1)S(1)} %bitcast.3) | data formatting | bytes 4194304
Async XLA Ops:
  101.2 2.5 %copy-start = (bf16[4,2,64,2048]{3,2,1,0:T(8,128)(2,1)S(1)}, bf16[4,2,64,2048]{3,2,1,0:T(8,128)(2,1)}, u32[]{:S(2)}) copy-start(bf16[4,2,64,2048]{3,2,1,0:T(8,128)(2,1)} %get-tuple-element.5) | copy-start | bytes 6291460

commit v3 on v2

--- a/solution.py
+++ b/solution.py
@@ -21,38 +21,38 @@
 TO_LOG2 = SIZE ** -0.5 * 1.4426950408889634
 
 ARRIVALS = (
-    ((16, 215, 109, 308, 301, 214, 307, 17, 102, 213, 306, 18, 212, 310, 211, 104, 305, 103, 20, 19),
-     (16, 308, 215, 109, 214, 110, 101, 213, 307, 17, 102, 212, 103, 18, 111, 19, 306, 205, 204, 20)),
-    ((16, 101, 308, 215, 117, 307, 110, 214, 302, 309, 213, 18, 212, 103, 19, 306, 211, 204, 305, 20),
-     (101, 16, 215, 17, 308, 214, 309, 110, 213, 111, 102, 307, 18, 306, 205, 103, 104, 19, 212, 120)),
-    ((101, 16, 308, 17, 215, 309, 102, 214, 18, 213, 111, 310, 212, 307, 303, 205, 306, 19, 304, 20),
-     (16, 101, 215, 102, 308, 17, 214, 18, 307, 109, 310, 206, 111, 112, 213, 103, 119, 205, 104, 120)),
-    ((101, 16, 17, 215, 308, 102, 214, 307, 18, 213, 103, 206, 309, 19, 310, 305, 212, 304, 111, 20),
-     (16, 101, 215, 308, 17, 102, 214, 307, 103, 18, 309, 19, 110, 206, 111, 213, 112, 205, 104, 120)),
-    ((101, 16, 215, 308, 17, 214, 207, 102, 213, 310, 18, 103, 206, 309, 19, 311, 204, 205, 20, 212),
-     (16, 101, 215, 117, 308, 307, 102, 309, 18, 103, 214, 310, 19, 104, 206, 111, 20, 112, 113, 205)),
-    ((16, 101, 215, 308, 102, 17, 307, 214, 18, 109, 205, 310, 103, 311, 19, 306, 104, 213, 112, 20),
-     (101, 16, 308, 17, 215, 102, 309, 207, 18, 310, 103, 205, 19, 214, 104, 213, 20, 311, 206, 112)),
-    ((16, 101, 308, 215, 206, 17, 102, 307, 103, 18, 310, 19, 214, 309, 213, 104, 311, 112, 20, 305),
-     (101, 16, 17, 308, 102, 309, 206, 18, 215, 214, 103, 307, 110, 19, 104, 311, 205, 20, 213, 112)),
-    ((16, 207, 101, 308, 17, 309, 102, 215, 18, 103, 214, 310, 104, 19, 111, 20, 213, 306, 105, 312),
-     (101, 16, 207, 17, 308, 102, 215, 18, 309, 103, 310, 19, 220, 306, 214, 311, 104, 105, 312, 213)),
-    ((308, 16, 215, 109, 317, 207, 101, 214, 102, 103, 18, 310, 19, 206, 213, 111, 205, 104, 320, 312),
-     (16, 308, 215, 101, 207, 102, 17, 18, 309, 206, 214, 103, 310, 104, 19, 320, 311, 205, 213, 112)),
-    ((16, 308, 101, 215, 109, 17, 110, 207, 318, 214, 102, 206, 103, 104, 19, 320, 213, 311, 205, 212),
-     (101, 16, 308, 17, 309, 207, 215, 102, 214, 103, 18, 19, 310, 206, 212, 104, 313, 111, 20, 105)),
-    ((16, 101, 308, 17, 309, 215, 102, 207, 110, 18, 214, 111, 319, 206, 103, 320, 212, 104, 213, 105),
-     (308, 16, 101, 215, 102, 207, 17, 309, 18, 310, 206, 103, 213, 104, 314, 19, 20, 311, 205, 112)),
-    ((101, 16, 308, 215, 17, 309, 102, 310, 18, 207, 206, 103, 311, 213, 112, 19, 314, 120, 205, 104),
-     (16, 308, 101, 109, 215, 17, 207, 214, 102, 310, 103, 18, 311, 19, 206, 104, 205, 20, 213, 112)),
-    ((16, 308, 101, 309, 207, 102, 17, 18, 214, 215, 103, 310, 19, 206, 311, 104, 113, 20, 312, 205),
-     (101, 16, 308, 215, 17, 309, 207, 102, 110, 18, 206, 103, 311, 112, 19, 214, 204, 205, 120, 213)),
-    ((308, 101, 16, 215, 17, 309, 207, 102, 310, 103, 18, 19, 214, 313, 104, 205, 311, 20, 112, 206),
-     (16, 308, 101, 309, 207, 102, 17, 18, 215, 310, 205, 103, 111, 19, 206, 313, 104, 214, 312, 20)),
-    ((16, 308, 101, 215, 102, 17, 309, 18, 314, 310, 206, 103, 207, 104, 19, 20, 213, 111, 105, 312),
-     (308, 101, 16, 17, 309, 206, 207, 102, 215, 103, 18, 19, 314, 310, 213, 104, 311, 20, 312, 105)),
-    ((16, 101, 207, 308, 17, 215, 309, 102, 103, 18, 310, 214, 19, 311, 104, 312, 105, 20, 213, 106),
-     (207, 308, 16, 101, 309, 102, 17, 215, 18, 310, 214, 103, 311, 104, 19, 213, 20, 105, 312, 106)),
+    ((16, 215, 308, 109, 214, 307, 101, 206, 102, 213, 17, 305, 18, 310, 212, 311, 204, 103, 20, 19),
+     (16, 308, 109, 215, 301, 110, 214, 17, 307, 102, 213, 306, 205, 103, 18, 112, 19, 304, 211, 20)),
+    ((16, 101, 308, 215, 117, 307, 214, 110, 213, 309, 102, 103, 305, 212, 18, 19, 306, 211, 204, 20),
+     (101, 16, 17, 308, 215, 110, 309, 214, 302, 111, 206, 18, 307, 212, 305, 213, 103, 104, 19, 120)),
+    ((16, 101, 308, 215, 17, 307, 214, 102, 109, 18, 306, 213, 111, 310, 212, 103, 305, 104, 19, 20),
+     (101, 16, 17, 308, 215, 102, 18, 307, 214, 213, 111, 309, 306, 212, 103, 305, 19, 210, 104, 120)),
+    ((16, 101, 308, 215, 17, 102, 307, 214, 18, 103, 309, 213, 110, 19, 205, 112, 311, 206, 104, 120),
+     (101, 16, 17, 308, 215, 102, 309, 214, 18, 103, 306, 213, 19, 310, 212, 311, 104, 305, 207, 20)),
+    ((16, 101, 308, 215, 17, 102, 307, 214, 18, 309, 103, 306, 204, 310, 19, 20, 311, 213, 205, 212),
+     (101, 16, 215, 17, 308, 102, 309, 214, 18, 103, 213, 19, 104, 207, 110, 20, 306, 111, 312, 205)),
+    ((101, 16, 17, 215, 308, 307, 102, 205, 309, 18, 103, 214, 306, 19, 104, 213, 110, 20, 212, 311),
+     (16, 101, 215, 308, 102, 17, 214, 18, 103, 205, 309, 19, 104, 213, 307, 311, 20, 206, 310, 112)),
+    ((101, 16, 308, 17, 206, 102, 18, 309, 215, 307, 103, 310, 214, 19, 104, 213, 311, 212, 20, 105),
+     (16, 101, 215, 308, 17, 307, 206, 102, 103, 18, 214, 19, 104, 310, 209, 311, 20, 105, 312, 213)),
+    ((207, 16, 101, 308, 102, 17, 309, 18, 215, 103, 214, 19, 213, 306, 104, 310, 212, 311, 20, 105),
+     (16, 101, 207, 308, 17, 215, 102, 309, 18, 310, 103, 306, 104, 19, 214, 20, 105, 213, 311, 212)),
+    ((308, 16, 215, 101, 207, 317, 102, 213, 103, 18, 309, 314, 19, 206, 310, 212, 104, 205, 111, 20),
+     (16, 308, 109, 207, 317, 102, 215, 318, 214, 206, 103, 101, 19, 212, 310, 104, 311, 20, 313, 205)),
+    ((16, 308, 101, 215, 109, 17, 214, 102, 207, 213, 318, 103, 104, 19, 206, 310, 20, 311, 212, 205),
+     (308, 101, 16, 17, 309, 215, 110, 207, 318, 103, 213, 319, 206, 314, 104, 212, 102, 20, 311, 105)),
+    ((16, 101, 308, 215, 17, 309, 214, 102, 207, 110, 18, 103, 213, 319, 206, 104, 212, 105, 320, 311),
+     (308, 16, 101, 309, 215, 102, 17, 18, 310, 214, 111, 207, 213, 319, 104, 320, 212, 105, 206, 103)),
+    ((16, 308, 101, 215, 102, 17, 309, 18, 207, 310, 214, 103, 111, 213, 19, 206, 104, 212, 320, 105),
+     (101, 16, 308, 17, 309, 215, 214, 102, 310, 103, 18, 19, 311, 207, 112, 213, 320, 105, 206, 204)),
+    ((16, 308, 101, 215, 17, 309, 214, 102, 207, 103, 18, 310, 19, 213, 311, 104, 206, 312, 20, 205),
+     (101, 16, 308, 215, 17, 309, 102, 18, 310, 207, 103, 311, 214, 104, 19, 20, 206, 112, 205, 113)),
+    ((101, 16, 308, 215, 17, 309, 207, 102, 214, 18, 310, 103, 313, 104, 19, 311, 206, 20, 205, 212),
+     (16, 308, 101, 215, 102, 17, 309, 18, 310, 103, 214, 19, 207, 313, 206, 104, 311, 105, 20, 312)),
+    ((16, 308, 101, 309, 215, 102, 17, 18, 314, 310, 207, 103, 206, 19, 213, 104, 311, 105, 20, 312),
+     (308, 101, 16, 215, 17, 309, 206, 102, 207, 103, 18, 314, 19, 310, 104, 311, 213, 20, 312, 105)),
+    ((308, 101, 16, 207, 17, 215, 309, 102, 310, 103, 214, 18, 19, 311, 220, 104, 312, 213, 105, 106),
+     (16, 207, 308, 101, 309, 102, 17, 215, 18, 214, 310, 103, 104, 19, 311, 20, 312, 213, 105, 106)),
 )
 
 
@@ -348,7 +348,6 @@
             arrive(0, half, j)
         if half == 0:
             first_leg()
-    second_leg()
 
     def step(k, carry):
         for half in range(2):
@@ -359,17 +358,14 @@
                 for j in range(4):
                     arrive(k + 1, half, j)
 
-        @pl.when(k == 1)
-        def _():
-            third_leg()
-
-        @pl.when(k == 3)
-        def _():
-            fourth_leg()
+            @pl.when(k == (3, 1)[half])
+            def _():
+                (third_leg, second_leg)[half]()
 
         return carry
 
     lax.fori_loop(0, 5, step, 0)
+    fourth_leg()
 
     for h in range(HEADS):
         denominator = jnp.sum(total[h], axis=1, keepdims=True)

time: 105 us -> 94.2 us (0.90)
  the two profiles are of different devices: /device:TPU:18 before, /device:TPU:105 now
where the time goes in v3:
time: 94.2 us; the launch traced here: 94.1 us
  Pallas kernels  89.6 us (95%)
  local copies, waits for them, and re-layouts  3.78 us (4%)
    pallas_call x1, Pallas kernels, on_device(): pl.pallas_call(kernel, out_shape=(jax.ShapeDtypeStruct((TOK, HEADS * SIZE...  89.6 us
    unnamed x4, local copies, waits for them, and re-layouts  3.78 us

profile of v3, /device:TPU:105, one launch (start us, length us, event | category | flops | bytes accessed | tf_op | source)
XLA Modules:
  0.0 94.1 jit_solution(11190665239420662055)
XLA Ops:
  0.6 89.6 %attend_and_send.1 = (bf16[256,2048]{1,0:T(8,128)(2,1)}, bf16[4,2,64,2048]{3,2,1,0:T(8,128)(2,1)}) custom-call(bf16[256,2048]{1,0:T(8,128)(2,1)} %q_hbm.1, bf16[256,256]{1,0:T(8,128)(2,1)} %k_hbm.1, bf16[256,256]{1,0:T(8,128)(2,1)} %v_hbm.1, s32[1,256]{1,0:T(1,128)} %bitcast.4, s32[1,256]{1,0:T(1,128)} %bitcast.5), custom_call_target="tpu_custom_call" | custom-call | flops 12000000000 | bytes 6000000 | tf_op jit(solution)/shard_map/attend_and_send/pallas_call | solution.py:401
  90.3 0.0 copy-start
  90.3 2.5 %copy.9 = bf16[256,2048]{1,0:T(8,128)(2,1)} copy(bf16[256,2048]{1,0:T(8,128)(2,1)} %get-tuple-element.8) | data formatting | bytes 2097152
  92.7 0.0 copy-done
  92.7 1.3 %copy.10 = bf16[512,2048]{1,0:T(8,128)(2,1)} copy(bf16[512,2048]{1,0:T(8,128)(2,1)S(1)} %bitcast.3) | data formatting | bytes 4194304
Async XLA Ops:
  90.3 2.5 %copy-start = (bf16[4,2,64,2048]{3,2,1,0:T(8,128)(2,1)S(1)}, bf16[4,2,64,2048]{3,2,1,0:T(8,128)(2,1)}, u32[]{:S(2)}) copy-start(bf16[4,2,64,2048]{3,2,1,0:T(8,128)(2,1)} %get-tuple-element.5) | copy-start | bytes 6291460

commit v4 on v3

--- a/solution.py
+++ b/solution.py
@@ -15,9 +15,8 @@
 REACH = 20
 SLOT = 8
 STEP = 4
-KEY_ROW, MASK_ROW, SENT_ROWS, ALL_ROWS = 128, 256, 272, 384
-FAR = 1024.0
-ROWS = 16
+KEY_ROW, ALL_ROWS = SIZE + 16, 2 * SIZE + 16
+HIDDEN = 1e30
 TO_LOG2 = SIZE ** -0.5 * 1.4426950408889634
 
 ARRIVALS = (
@@ -91,9 +90,10 @@
 
 
 def kernel(q_hbm, k_hbm, v_hbm, seg_hbm, own_hbm, out_ref, cache_ref,
-           q_aug, k_own, v_own, seg_ref, own_ref, kv, bias, top, total, acc, scores_a, scores_b, weights_a, weights_b, shrink_a, shrink_b,
+           q_own, q_turned, k_own, v_own, own_values, seg_ref, own_ref, kv, bias, top, acc, scores_a, scores_b, weights_a, weights_b,
+           peaks_a, peaks_b, shrink_a, shrink_b,
            outgoing, mid, recv, block,
-           in_sem, q_sem, kv_send, kv_recv, z_send, z_recv, x_send, x_recv, y_send, y_recv, c_send, c_recv, own_sem):
+           in_sem, kv_send, kv_recv, z_send, z_recv, x_send, x_recv, y_send, y_recv, c_send, c_recv, own_sem):
     me, g = lax.axis_index("inst"), lax.axis_index("head")
     kind = me % 16
     x, y, z = me // 16, (me // 8) % 2, me % 8
@@ -108,12 +108,10 @@
 
     inputs = [
         pltpu.make_async_copy(src, dst, in_sem.at[n])
-        for n, (src, dst) in enumerate(((k_hbm, k_own), (v_hbm, v_own), (seg_hbm, seg_ref), (own_hbm, own_ref)))
+        for n, (src, dst) in enumerate(
+            ((k_hbm, k_own), (v_hbm, v_own), (seg_hbm, seg_ref), (own_hbm, own_ref), (q_hbm, q_own)))
     ]
-    queries = [
-        pltpu.make_async_copy(q_hbm.at[:, h * SIZE:(h + 1) * SIZE], q_aug.at[h, :, 0:SIZE], q_sem.at[h]) for h in range(HEADS)
-    ]
-    for copy in inputs + queries:
+    for copy in inputs:
         copy.start()
 
     def along_z(by):
@@ -156,8 +154,8 @@
             @pl.when(there > 0)
             def _():
                 copy = pltpu.make_async_remote_copy(
-                    src_ref=kv.at[half, slot, 0:SENT_ROWS],
-                    dst_ref=kv.at[half, there, 0:SENT_ROWS],
+                    src_ref=kv.at[half, slot],
+                    dst_ref=kv.at[half, there],
                     send_sem=kv_send.at[half * 4 + link, slot],
                     recv_sem=kv_recv.at[half, there],
                     device_id=(near[link], g),
@@ -171,31 +169,40 @@
     def arrive(k, h, j):
         half, jj = j % 2, 2 * h + j // 2
         slot = STEP * k + jj + 1
-        here = kv.at[half, slot, 0:SENT_ROWS]
+        here = kv.at[half, slot]
         pltpu.make_async_copy(here, here, kv_recv.at[half, slot]).wait()
         forward(half, slot, digits(half, jj, k))
 
     for copy in inputs[:3]:
         copy.wait()
+    at0 = lax.broadcasted_iota(jnp.int32, (TOK, TOK), 0)
+    at1 = lax.broadcasted_iota(jnp.int32, (TOK, TOK), 1)
     seg_row = seg_ref[...].astype(F32)
     seg_wide = jnp.broadcast_to(seg_row, (TOK, TOK))
-    request = lax.broadcasted_iota(jnp.int32, (16, TOK), 0).astype(F32)
+    seg_tall = jnp.broadcast_to(jnp.sum(jnp.where(at0 == at1, seg_wide, 0.0), axis=1, keepdims=True), (TOK, TOK))
+    first_seg, last_seg = jnp.min(seg_tall, axis=0, keepdims=True), jnp.max(seg_tall, axis=0, keepdims=True)
+    reaches = (seg_row == last_seg).astype(F32)
+    extra = lax.broadcasted_iota(jnp.int32, (16, TOK), 0)
+    extra_rows = jnp.where(extra == 0, reaches, jnp.where(extra == 1, last_seg, 0.0)).astype(BF16)
     for half in range(2):
         feat = slice(half * SIZE, (half + 1) * SIZE)
-        kv[half, 0, 0:KEY_ROW, 0:SIZE] = v_own[0:SIZE, feat]
-        kv[half, 0, 0:KEY_ROW, SIZE:TOK] = v_own[SIZE:TOK, feat]
-        kv[half, 0, KEY_ROW:MASK_ROW, :] = k_own[:, feat].astype(F32).T.astype(BF16)
-        kv[half, 0, MASK_ROW:SENT_ROWS, :] = jnp.where(seg_wide[0:16] == request, 0.0, -FAR).astype(BF16)
+        turned = v_own[:, feat].astype(F32).T
+        own_values[half, 0:SIZE, :] = turned.astype(BF16)
+        own_values[half, SIZE:KEY_ROW, :] = jnp.where(extra == 0, 1.0, 0.0).astype(BF16)
+        kv[half, 0, 0:SIZE, :] = (turned * reaches).astype(BF16)
+        kv[half, 0, SIZE:KEY_ROW, :] = extra_rows
+        keys = k_own[:, feat].astype(F32)
+        last_key = jnp.broadcast_to(keys[TOK - 1:TOK, :], (TOK, SIZE))
+        keys = jnp.where(seg_tall[:, 0:SIZE] == last_seg[:, 0:SIZE], keys, last_key).astype(BF16)
+        kv[half, 0, KEY_ROW:ALL_ROWS, 0:SIZE] = keys[0:SIZE]
+        kv[half, 0, KEY_ROW:ALL_ROWS, SIZE:TOK] = keys[SIZE:TOK]
+    inputs[4].wait()
+    for h in range(HEADS):
+        q_turned[h] = q_own[:, h * SIZE:(h + 1) * SIZE].astype(F32).T.astype(BF16)
+    bias[...] = jnp.where((at0 <= at1) & (seg_tall == seg_wide), 0.0, -HIDDEN)
     pl.semaphore_wait(barrier, len(partners))
     forward(0, 0, first[0])
     forward(1, 0, first[1])
-
-    def clear(slot, carry):
-        for half in range(2):
-            kv[half, slot, SENT_ROWS:ALL_ROWS, :] = jnp.zeros((ALL_ROWS - SENT_ROWS, TOK), BF16)
-        return carry
-
-    lax.fori_loop(0, REACH + 1, clear, 0)
 
     inputs[3].wait()
     dest = own_ref[...]
@@ -284,92 +291,98 @@
             pltpu.make_async_copy(here, here, y_recv.at[n]).wait()
             c_copy(n).start()
 
-    at0 = lax.broadcasted_iota(jnp.int32, (TOK, TOK), 0)
-    at1 = lax.broadcasted_iota(jnp.int32, (TOK, TOK), 1)
-    seg_col = jnp.sum(jnp.where(at0 == at1, seg_wide, 0.0), axis=1, keepdims=True)
-    lane = lax.broadcasted_iota(jnp.int32, (TOK, SIZE), 1).astype(F32)
-    query_mask = jnp.where(lane == seg_col, FAR, 0.0).astype(BF16)
-    for h in range(HEADS):
-        q_aug[h, :, SIZE:2 * SIZE] = query_mask
-    bias[...] = jnp.where(at0 >= at1, 0.0, -1e30)
-    scores_of, weights_of, shrink_of = (scores_a, scores_b), (weights_a, weights_b), (shrink_a, shrink_b)
-
-    def unit(half, slots, diagonal):
-        width = len(slots) * TOK
-
-        def score(i, c):
-            scores_of[i % 2][:, c * TOK:(c + 1) * TOK] = jnp.dot(
-                q_aug[half * RATIO + i], kv[half, slots[c], KEY_ROW:ALL_ROWS, :], preferred_element_type=F32)
-
-        def soften(i, at):
-            h, rows = half * RATIO + i, slice(at, at + ROWS)
-            parts = [scores_of[i % 2][rows, j:j + SIZE] for j in range(0, width, SIZE)]
-            if diagonal:
-                parts = [part + bias[rows, n * SIZE:(n + 1) * SIZE] for n, part in enumerate(parts)]
-            largest = jnp.max(functools.reduce(jnp.maximum, parts), axis=1, keepdims=True)
-            if diagonal:
-                peak = jnp.broadcast_to(largest, (ROWS, SIZE))
-            else:
-                old = top[h, rows, :]
-                peak = jnp.maximum(old, largest)
-                shrink = jnp.exp2((old - peak) * TO_LOG2)
-                shrink_of[i % 2][rows, :] = shrink
-            weights = [jnp.exp2((part - peak) * TO_LOG2) for part in parts]
-            for n, weight in enumerate(weights):
-                weights_of[i % 2][rows, n * SIZE:(n + 1) * SIZE] = weight.astype(BF16)
-            added = functools.reduce(jnp.add, weights)
-            top[h, rows, :] = peak
-            total[h, rows, :] = added if diagonal else total[h, rows, :] * shrink + added
-
-        def combine(i):
-            h = half * RATIO + i
-            values = jnp.concatenate(
-                [kv[half, slot, 0:KEY_ROW, lanes:lanes + SIZE] for slot in slots for lanes in (0, SIZE)], axis=0)
-            product = jnp.dot(weights_of[i % 2][:, 0:width], values, preferred_element_type=F32)
-            acc[h] = product if diagonal else acc[h] * shrink_of[i % 2][...] + product
-
+    scores_of, weights_of = (scores_a, scores_b), (weights_a, weights_b)
+    peaks_of, shrink_of = (peaks_a, peaks_b), (shrink_a, shrink_b)
+
+    def score(n, h, slots):
+        if slots is None:
+            keys = k_own[:, (h // RATIO) * SIZE:(h // RATIO + 1) * SIZE]
+        else:
+            keys = jnp.concatenate(
+                [kv[h // RATIO, slot, KEY_ROW:ALL_ROWS, lanes:lanes + SIZE] for slot in slots for lanes in (0, SIZE)], axis=0)
+        product = jnp.dot(keys, q_turned[h], preferred_element_type=F32)
+        if slots is None:
+            product += bias[...]
+        scores_of[n % 2][0:product.shape[0], :] = product
+        for c in range(product.shape[0] // TOK):
+            peaks_of[n % 2][c] = jnp.max(product[c * TOK:(c + 1) * TOK], axis=0, keepdims=True)
+
+    def peak_rows(n, h, slots):
+        if slots is None:
+            top[h] = peaks_of[n % 2][0]
+            return [top[h]]
+        seen = []
+        for slot in slots:
+            block_seg = kv[h // RATIO, slot, SIZE:KEY_ROW, :].astype(F32)[1:2, :]
+            seen.append((block_seg == first_seg) & (seg_row == first_seg))
+        old = top[h]
+        peak = old
         for c in range(len(slots)):
-            score(0, c)
-        for i in range(RATIO):
-            for quarter in range(4):
-                if i + 1 < RATIO and quarter < len(slots):
-                    score(i + 1, quarter)
-                for at in range(quarter * 64, quarter * 64 + 64, ROWS):
-                    soften(i, at)
-                if quarter == 1 and i > 0:
-                    combine(i - 1)
-        combine(RATIO - 1)
-
-    for copy in queries:
-        copy.wait()
+            peak = jnp.maximum(peak, jnp.where(seen[c], peaks_of[n % 2][c], -HIDDEN))
+        top[h] = peak
+        shrink_of[n % 2][...] = jnp.exp2((old - peak) * TO_LOG2)
+        return [jnp.where(seen[c], peak, HIDDEN) for c in range(len(slots))]
+
+    def soften(n, peaks, c, start, rows):
+        at = slice(c * TOK + start, c * TOK + start + rows)
+        weights_of[n % 2][at, :] = jnp.exp2((scores_of[n % 2][at, :] - peaks[c]) * TO_LOG2).astype(BF16)
+
+    def combine(n, h, slots):
+        if slots is None:
+            acc[h] = jnp.dot(own_values[h // RATIO], weights_of[n % 2][0:TOK, :], preferred_element_type=F32)
+        else:
+            values = jnp.concatenate([kv[h // RATIO, slot, 0:KEY_ROW, :] for slot in slots], axis=1)
+            product = jnp.dot(values, weights_of[n % 2][...], preferred_element_type=F32)
+            acc[h] = acc[h] * shrink_of[n % 2][...] + product
+
+    def turn(n, before, now, after):
+        peaks = peak_rows(n, *now)
+        if before is not None:
+            combine(n - 1, *before)
+        for c in range(len(peaks)):
+            if after is not None and c == len(peaks) // 2:
+                score(n + 1, *after)
+            for start in range(0, TOK, 64):
+                soften(n, peaks, c, start, 64)
+
     for half in range(2):
-        unit(half, [0], True)
+        heads = [(half * RATIO + i, None) for i in range(RATIO)]
+        score(0, *heads[0])
+        for n in range(RATIO):
+            turn(n, heads[n - 1] if n > 0 else None, heads[n], heads[n + 1] if n + 1 < RATIO else None)
+        combine(RATIO - 1, *heads[-1])
         for j in range(4):
             arrive(0, half, j)
         if half == 0:
             first_leg()
 
+    def slots_of(k):
+        return [STEP * k + 1 + c for c in range(STEP)]
+
+    score(0, 0, slots_of(0))
+
     def step(k, carry):
-        for half in range(2):
-            unit(half, [STEP * k + 1 + c for c in range(STEP)], False)
-
-            @pl.when(k < 4)
-            def _():
-                for j in range(4):
-                    arrive(k + 1, half, j)
-
-            @pl.when(k == (3, 1)[half])
-            def _():
-                (third_leg, second_leg)[half]()
-
+        now = slots_of(k)
+        turns = [(h, now) for h in range(HEADS)] + [(0, slots_of(jnp.minimum(k + 1, 4)))]
+        for n in range(HEADS):
+            turn(n, turns[n - 1] if n > 0 else None, turns[n], turns[n + 1])
+            if n == HEADS - 1:
+                combine(n, *turns[n])
+            if n % 2 == 1:
+                @pl.when(k < 4)
+                def _():
+                    arrive(k + 1, n // 8, (n // 2) % 4)
+            if n % 8 == 7:
+                @pl.when(k == (3, 1)[n // 8])
+                def _():
+                    (third_leg, second_leg)[n // 8]()
         return carry
 
     lax.fori_loop(0, 5, step, 0)
     fourth_leg()
 
     for h in range(HEADS):
-        denominator = jnp.sum(total[h], axis=1, keepdims=True)
-        out_ref[:, h * SIZE:(h + 1) * SIZE] = (acc[h] / denominator).astype(BF16)
+        out_ref[:, h * SIZE:(h + 1) * SIZE] = (acc[h, 0:SIZE, :] / acc[h, SIZE:SIZE + 1, :]).T.astype(BF16)
 
     for half in range(2):
         forward(half, 0, first[half], wait=True)
@@ -407,28 +420,30 @@
         in_specs=[whole] * 5,
         out_specs=(pl.BlockSpec(memory_space=pltpu.VMEM), whole),
         scratch_shapes=[
-            pltpu.VMEM((HEADS, TOK, 2 * SIZE), BF16),
+            pltpu.VMEM((TOK, HEADS * SIZE), BF16),
+            pltpu.VMEM((HEADS, SIZE, TOK), BF16),
             pltpu.VMEM((TOK, 2 * SIZE), BF16),
             pltpu.VMEM((TOK, 2 * SIZE), BF16),
+            pltpu.VMEM((2, KEY_ROW, TOK), BF16),
             pltpu.VMEM((1, TOK), jnp.int32),
             pltpu.VMEM((1, TOK), jnp.int32),
             pltpu.VMEM((2, REACH + 1, ALL_ROWS, TOK), BF16),
             pltpu.VMEM((TOK, TOK), F32),
-            pltpu.VMEM((HEADS, TOK, SIZE), F32),
-            pltpu.VMEM((HEADS, TOK, SIZE), F32),
-            pltpu.VMEM((HEADS, TOK, SIZE), F32),
-            pltpu.VMEM((TOK, STEP * TOK), F32),
-            pltpu.VMEM((TOK, STEP * TOK), F32),
-            pltpu.VMEM((TOK, STEP * TOK), BF16),
-            pltpu.VMEM((TOK, STEP * TOK), BF16),
-            pltpu.VMEM((TOK, SIZE), F32),
-            pltpu.VMEM((TOK, SIZE), F32),
+            pltpu.VMEM((HEADS, 1, TOK), F32),
+            pltpu.VMEM((HEADS, KEY_ROW, TOK), F32),
+            pltpu.VMEM((STEP * TOK, TOK), F32),
+            pltpu.VMEM((STEP * TOK, TOK), F32),
+            pltpu.VMEM((STEP * TOK, TOK), BF16),
+            pltpu.VMEM((STEP * TOK, TOK), BF16),
+            pltpu.VMEM((STEP, 1, TOK), F32),
+            pltpu.VMEM((STEP, 1, TOK), F32),
+            pltpu.VMEM((1, TOK), F32),
+            pltpu.VMEM((1, TOK), F32),
             pltpu.VMEM((4, 2, 8, 2 * SLOT, 2 * SIZE), BF16),
             pltpu.VMEM((8, 4, 2, 2 * SLOT, 2 * SIZE), BF16),
             pltpu.VMEM((4, 8, 2, 2 * SLOT, 2 * SIZE), BF16),
             pltpu.VMEM((2, 4, 64, 4 * SIZE), BF16),
-            pltpu.SemaphoreType.DMA((4,)),
-            pltpu.SemaphoreType.DMA((HEADS,)),
+            pltpu.SemaphoreType.DMA((5,)),
             pltpu.SemaphoreType.DMA((8, REACH + 1)),
             pltpu.SemaphoreType.DMA((2, REACH + 1)),
             pltpu.SemaphoreType.DMA((8,)),

time: 94.2 us -> 91.7 us (0.973)
  the two profiles are of different devices: /device:TPU:105 before, /device:TPU:1 now
where the time goes in v4:
time: 91.7 us; the launch traced here: 90.2 us
  Pallas kernels  85.8 us (94%)
  local copies, waits for them, and re-layouts  3.78 us (4%)
    pallas_call x1, Pallas kernels, on_device(): pl.pallas_call(kernel, out_shape=(jax.ShapeDtypeStruct((TOK, HEADS * SIZE...  85.8 us
    unnamed x4, local copies, waits for them, and re-layouts  3.78 us

profile of v4, /device:TPU:1, one launch (start us, length us, event | category | flops | bytes accessed | tf_op | source)
XLA Modules:
  0.0 90.2 jit_solution(52695092382932598)
XLA Ops:
  0.6 85.8 %attend_and_send.1 = (bf16[256,2048]{1,0:T(8,128)(2,1)}, bf16[4,2,64,2048]{3,2,1,0:T(8,128)(2,1)}) custom-call(bf16[256,2048]{1,0:T(8,128)(2,1)} %q_hbm.1, bf16[256,256]{1,0:T(8,128)(2,1)} %k_hbm.1, bf16[256,256]{1,0:T(8,128)(2,1)} %v_hbm.1, s32[1,256]{1,0:T(1,128)} %bitcast.4, s32[1,256]{1,0:T(1,128)} %bitcast.5), custom_call_target="tpu_custom_call" | custom-call | flops 12000000000 | bytes 6000000 | tf_op jit(solution)/shard_map/attend_and_send/pallas_call | solution.py:414
  86.4 0.0 copy-start
  86.4 2.5 %copy.9 = bf16[256,2048]{1,0:T(8,128)(2,1)} copy(bf16[256,2048]{1,0:T(8,128)(2,1)} %get-tuple-element.8) | data formatting | bytes 2097152
  88.9 0.0 copy-done
  88.9 1.3 %copy.10 = bf16[512,2048]{1,0:T(8,128)(2,1)} copy(bf16[512,2048]{1,0:T(8,128)(2,1)S(1)} %bitcast.3) | data formatting | bytes 4194304
Async XLA Ops:
  86.4 2.5 %copy-start = (bf16[4,2,64,2048]{3,2,1,0:T(8,128)(2,1)S(1)}, bf16[4,2,64,2048]{3,2,1,0:T(8,128)(2,1)}, u32[]{:S(2)}) copy-start(bf16[4,2,64,2048]{3,2,1,0:T(8,128)(2,1)} %get-tuple-element.5) | copy-start | bytes 6291460

commit v5 on v4

--- a/solution.py
+++ b/solution.py
@@ -20,38 +20,38 @@
 TO_LOG2 = SIZE ** -0.5 * 1.4426950408889634
 
 ARRIVALS = (
-    ((16, 215, 308, 109, 214, 307, 101, 206, 102, 213, 17, 305, 18, 310, 212, 311, 204, 103, 20, 19),
-     (16, 308, 109, 215, 301, 110, 214, 17, 307, 102, 213, 306, 205, 103, 18, 112, 19, 304, 211, 20)),
-    ((16, 101, 308, 215, 117, 307, 214, 110, 213, 309, 102, 103, 305, 212, 18, 19, 306, 211, 204, 20),
-     (101, 16, 17, 308, 215, 110, 309, 214, 302, 111, 206, 18, 307, 212, 305, 213, 103, 104, 19, 120)),
-    ((16, 101, 308, 215, 17, 307, 214, 102, 109, 18, 306, 213, 111, 310, 212, 103, 305, 104, 19, 20),
-     (101, 16, 17, 308, 215, 102, 18, 307, 214, 213, 111, 309, 306, 212, 103, 305, 19, 210, 104, 120)),
-    ((16, 101, 308, 215, 17, 102, 307, 214, 18, 103, 309, 213, 110, 19, 205, 112, 311, 206, 104, 120),
-     (101, 16, 17, 308, 215, 102, 309, 214, 18, 103, 306, 213, 19, 310, 212, 311, 104, 305, 207, 20)),
-    ((16, 101, 308, 215, 17, 102, 307, 214, 18, 309, 103, 306, 204, 310, 19, 20, 311, 213, 205, 212),
-     (101, 16, 215, 17, 308, 102, 309, 214, 18, 103, 213, 19, 104, 207, 110, 20, 306, 111, 312, 205)),
-    ((101, 16, 17, 215, 308, 307, 102, 205, 309, 18, 103, 214, 306, 19, 104, 213, 110, 20, 212, 311),
-     (16, 101, 215, 308, 102, 17, 214, 18, 103, 205, 309, 19, 104, 213, 307, 311, 20, 206, 310, 112)),
-    ((101, 16, 308, 17, 206, 102, 18, 309, 215, 307, 103, 310, 214, 19, 104, 213, 311, 212, 20, 105),
-     (16, 101, 215, 308, 17, 307, 206, 102, 103, 18, 214, 19, 104, 310, 209, 311, 20, 105, 312, 213)),
-    ((207, 16, 101, 308, 102, 17, 309, 18, 215, 103, 214, 19, 213, 306, 104, 310, 212, 311, 20, 105),
-     (16, 101, 207, 308, 17, 215, 102, 309, 18, 310, 103, 306, 104, 19, 214, 20, 105, 213, 311, 212)),
-    ((308, 16, 215, 101, 207, 317, 102, 213, 103, 18, 309, 314, 19, 206, 310, 212, 104, 205, 111, 20),
-     (16, 308, 109, 207, 317, 102, 215, 318, 214, 206, 103, 101, 19, 212, 310, 104, 311, 20, 313, 205)),
-    ((16, 308, 101, 215, 109, 17, 214, 102, 207, 213, 318, 103, 104, 19, 206, 310, 20, 311, 212, 205),
-     (308, 101, 16, 17, 309, 215, 110, 207, 318, 103, 213, 319, 206, 314, 104, 212, 102, 20, 311, 105)),
-    ((16, 101, 308, 215, 17, 309, 214, 102, 207, 110, 18, 103, 213, 319, 206, 104, 212, 105, 320, 311),
-     (308, 16, 101, 309, 215, 102, 17, 18, 310, 214, 111, 207, 213, 319, 104, 320, 212, 105, 206, 103)),
-    ((16, 308, 101, 215, 102, 17, 309, 18, 207, 310, 214, 103, 111, 213, 19, 206, 104, 212, 320, 105),
-     (101, 16, 308, 17, 309, 215, 214, 102, 310, 103, 18, 19, 311, 207, 112, 213, 320, 105, 206, 204)),
-    ((16, 308, 101, 215, 17, 309, 214, 102, 207, 103, 18, 310, 19, 213, 311, 104, 206, 312, 20, 205),
-     (101, 16, 308, 215, 17, 309, 102, 18, 310, 207, 103, 311, 214, 104, 19, 20, 206, 112, 205, 113)),
-    ((101, 16, 308, 215, 17, 309, 207, 102, 214, 18, 310, 103, 313, 104, 19, 311, 206, 20, 205, 212),
-     (16, 308, 101, 215, 102, 17, 309, 18, 310, 103, 214, 19, 207, 313, 206, 104, 311, 105, 20, 312)),
-    ((16, 308, 101, 309, 215, 102, 17, 18, 314, 310, 207, 103, 206, 19, 213, 104, 311, 105, 20, 312),
-     (308, 101, 16, 215, 17, 309, 206, 102, 207, 103, 18, 314, 19, 310, 104, 311, 213, 20, 312, 105)),
-    ((308, 101, 16, 207, 17, 215, 309, 102, 310, 103, 214, 18, 19, 311, 220, 104, 312, 213, 105, 106),
-     (16, 207, 308, 101, 309, 102, 17, 215, 18, 214, 310, 103, 104, 19, 311, 20, 312, 213, 105, 106)),
+    ((16, 109, 308, 215, 214, 101, 307, 17, 206, 102, 310, 205, 103, 18, 19, 311, 204, 113, 312, 20),
+     (16, 215, 109, 308, 307, 214, 101, 102, 17, 310, 206, 18, 311, 205, 103, 104, 19, 312, 213, 20)),
+    ((101, 16, 215, 17, 308, 110, 207, 309, 102, 306, 18, 213, 212, 305, 103, 104, 19, 311, 20, 214),
+     (16, 101, 308, 215, 17, 309, 110, 207, 214, 102, 306, 103, 18, 19, 205, 311, 213, 104, 312, 20)),
+    ((101, 16, 308, 102, 17, 215, 307, 18, 214, 111, 213, 306, 310, 103, 205, 19, 109, 212, 304, 20),
+     (101, 16, 215, 308, 102, 17, 214, 109, 307, 18, 111, 206, 212, 305, 103, 310, 304, 19, 213, 20)),
+    ((101, 16, 308, 102, 17, 215, 214, 103, 18, 307, 19, 206, 310, 112, 213, 311, 109, 204, 305, 20),
+     (16, 101, 215, 308, 102, 17, 309, 207, 103, 18, 213, 306, 110, 19, 311, 112, 214, 205, 304, 20)),
+    ((101, 16, 215, 308, 102, 17, 309, 103, 18, 207, 214, 104, 19, 310, 305, 111, 20, 212, 306, 213),
+     (16, 101, 215, 308, 102, 17, 214, 309, 103, 18, 306, 204, 110, 19, 213, 305, 107, 20, 212, 311)),
+    ((16, 101, 102, 215, 308, 17, 103, 18, 214, 307, 104, 19, 213, 105, 20, 309, 210, 312, 206, 311),
+     (101, 16, 215, 308, 17, 102, 205, 307, 103, 18, 214, 309, 306, 104, 19, 213, 311, 212, 110, 20)),
+    ((101, 16, 215, 308, 102, 17, 309, 103, 214, 18, 104, 19, 310, 207, 311, 105, 20, 206, 213, 312),
+     (101, 16, 206, 308, 102, 17, 215, 18, 309, 103, 214, 310, 213, 104, 19, 311, 107, 20, 312, 205)),
+    ((16, 207, 101, 308, 215, 102, 17, 309, 103, 18, 310, 104, 214, 19, 213, 20, 306, 111, 212, 305),
+     (207, 101, 16, 102, 17, 308, 309, 215, 103, 18, 214, 19, 310, 111, 306, 104, 213, 305, 20, 212)),
+    ((16, 308, 101, 17, 215, 207, 102, 309, 206, 18, 103, 212, 310, 19, 104, 314, 20, 213, 105, 311),
+     (308, 16, 215, 207, 101, 102, 17, 18, 103, 309, 206, 310, 19, 104, 205, 20, 211, 112, 313, 314)),
+    ((308, 101, 16, 207, 309, 102, 17, 214, 18, 315, 213, 103, 310, 19, 104, 206, 20, 105, 211, 312),
+     (308, 101, 16, 17, 207, 309, 102, 214, 103, 18, 315, 19, 206, 104, 212, 310, 20, 105, 211, 313)),
+    ((308, 101, 16, 215, 309, 17, 102, 214, 310, 103, 18, 19, 207, 104, 212, 311, 20, 105, 206, 313),
+     (308, 101, 16, 102, 215, 309, 17, 18, 207, 310, 103, 213, 104, 19, 212, 314, 20, 105, 311, 206)),
+    ((16, 308, 101, 215, 309, 102, 207, 17, 310, 18, 103, 311, 104, 213, 19, 314, 20, 105, 206, 212),
+     (308, 101, 16, 17, 309, 102, 214, 103, 207, 310, 18, 213, 19, 315, 104, 206, 105, 212, 311, 20)),
+    ((308, 101, 16, 309, 17, 102, 310, 103, 214, 18, 213, 311, 19, 315, 104, 207, 112, 20, 205, 206),
+     (308, 101, 16, 215, 102, 207, 309, 17, 214, 18, 310, 103, 104, 213, 19, 312, 20, 206, 311, 105)),
+    ((308, 101, 16, 102, 215, 309, 17, 214, 310, 18, 103, 206, 311, 104, 19, 207, 312, 20, 105, 213),
+     (101, 16, 308, 215, 309, 17, 102, 103, 214, 310, 18, 19, 207, 311, 104, 105, 213, 312, 20, 206)),
+    ((308, 101, 16, 215, 17, 309, 102, 207, 103, 214, 310, 18, 311, 19, 104, 213, 312, 105, 20, 206),
+     (16, 308, 101, 309, 102, 215, 17, 310, 18, 103, 207, 104, 214, 311, 19, 20, 213, 312, 105, 206)),
+    ((308, 16, 207, 101, 102, 309, 215, 17, 18, 310, 103, 214, 104, 213, 311, 19, 312, 20, 105, 106),
+     (207, 101, 308, 16, 309, 215, 17, 102, 310, 214, 103, 18, 311, 19, 104, 213, 105, 20, 312, 106)),
 )
 
 
@@ -136,14 +136,6 @@
         return chosen
 
     first = [[pick([TABLE[t][half][0][link] for t in range(16)]) for link in range(4)] for half in range(2)]
-    codes = [
-        [
-            [pick([sum(TABLE[t][half][STEP * k + jj + 1][link] * 64 ** k for k in range(5)) for t in range(16)]) for link in range(4)]
-            for jj in range(STEP)
-        ]
-        for half in range(2)
-    ]
-
     def digits(half, jj, k):
         return [(codes[half][jj][link] >> (6 * k)) & 63 for link in range(4)]
 
@@ -173,6 +165,9 @@
         pltpu.make_async_copy(here, here, kv_recv.at[half, slot]).wait()
         forward(half, slot, digits(half, jj, k))
 
+    def drain(k, half, jj):
+        forward(half, STEP * k + jj + 1, digits(half, jj, k), wait=True)
+
     for copy in inputs[:3]:
         copy.wait()
     at0 = lax.broadcasted_iota(jnp.int32, (TOK, TOK), 0)
@@ -187,8 +182,6 @@
     for half in range(2):
         feat = slice(half * SIZE, (half + 1) * SIZE)
         turned = v_own[:, feat].astype(F32).T
-        own_values[half, 0:SIZE, :] = turned.astype(BF16)
-        own_values[half, SIZE:KEY_ROW, :] = jnp.where(extra == 0, 1.0, 0.0).astype(BF16)
         kv[half, 0, 0:SIZE, :] = (turned * reaches).astype(BF16)
         kv[half, 0, SIZE:KEY_ROW, :] = extra_rows
         keys = k_own[:, feat].astype(F32)
@@ -196,13 +189,25 @@
         keys = jnp.where(seg_tall[:, 0:SIZE] == last_seg[:, 0:SIZE], keys, last_key).astype(BF16)
         kv[half, 0, KEY_ROW:ALL_ROWS, 0:SIZE] = keys[0:SIZE]
         kv[half, 0, KEY_ROW:ALL_ROWS, SIZE:TOK] = keys[SIZE:TOK]
+    pl.semaphore_wait(barrier, len(partners))
+    forward(0, 0, first[0])
+    forward(1, 0, first[1])
+
+    codes = [
+        [
+            [pick([sum(TABLE[t][half][STEP * k + jj + 1][link] * 64 ** k for k in range(5)) for t in range(16)]) for link in range(4)]
+            for jj in range(STEP)
+        ]
+        for half in range(2)
+    ]
+
+    for half in range(2):
+        own_values[half, 0:SIZE, :] = v_own[:, half * SIZE:(half + 1) * SIZE].astype(F32).T.astype(BF16)
+        own_values[half, SIZE:KEY_ROW, :] = jnp.where(extra == 0, 1.0, 0.0).astype(BF16)
     inputs[4].wait()
     for h in range(HEADS):
         q_turned[h] = q_own[:, h * SIZE:(h + 1) * SIZE].astype(F32).T.astype(BF16)
     bias[...] = jnp.where((at0 <= at1) & (seg_tall == seg_wide), 0.0, -HIDDEN)
-    pl.semaphore_wait(barrier, len(partners))
-    forward(0, 0, first[0])
-    forward(1, 0, first[1])
 
     inputs[3].wait()
     dest = own_ref[...]
@@ -372,6 +377,10 @@
                 @pl.when(k < 4)
                 def _():
                     arrive(k + 1, n // 8, (n // 2) % 4)
+
+                @pl.when(k > 0)
+                def _():
+                    drain(k - 1, n // 8, (n // 2) % 4)
             if n % 8 == 7:
                 @pl.when(k == (3, 1)[n // 8])
                 def _():
@@ -382,18 +391,12 @@
     fourth_leg()
 
     for h in range(HEADS):
-        out_ref[:, h * SIZE:(h + 1) * SIZE] = (acc[h, 0:SIZE, :] / acc[h, SIZE:SIZE + 1, :]).T.astype(BF16)
+        out_ref[:, h * SIZE:(h + 1) * SIZE] = (acc[h, 0:SIZE, :] * (1.0 / acc[h, SIZE:SIZE + 1, :])).T.astype(BF16)
 
     for half in range(2):
         forward(half, 0, first[half], wait=True)
-
-    def drain(k, carry):
-        for half in range(2):
-            for jj in range(STEP):
-                forward(half, STEP * k + jj + 1, digits(half, jj, k), wait=True)
-        return carry
-
-    lax.fori_loop(0, 5, drain, 0)
+        for jj in range(STEP):
+            drain(4, half, jj)
     for by in range(1, 8):
         z_copy(by).wait_send()
     for by in range(1, 4):
@@ -411,6 +414,7 @@
 
 def on_device(queries, keys, values, segments, owners):
     whole = pl.BlockSpec(memory_space=pl.ANY)
+    operands = (queries, keys, values, segments.reshape(1, TOK), owners.reshape(1, TOK))
     attended, cache = pl.pallas_call(
         kernel,
         out_shape=(
@@ -457,11 +461,11 @@
             pltpu.SemaphoreType.DMA(()),
         ],
         compiler_params=pltpu.CompilerParams(
-            collective_id=0, has_side_effects=True, vmem_limit_bytes=56 * 1024 * 1024
+            collective_id=0, has_side_effects=True, vmem_limit_bytes=40 * 1024 * 1024
         ),
         cost_estimate=pl.CostEstimate(flops=12_000_000_000, bytes_accessed=6_000_000, transcendentals=22_000_000),
         name="attend_and_send",
-    )(queries, keys, values, segments.reshape(1, TOK), owners.reshape(1, TOK))
+    )(*(pltpu.with_memory_space_constraint(a, pltpu.HBM) for a in operands))
     return attended, cache.reshape(64 * SLOT, 2048)
 
 

time: 91.7 us -> 97.5 us (1.063); the launches traced: 90.2 us -> 97.4 us
  Pallas kernels: 85.8 us -> 94.5 us
  local copies, waits for them, and re-layouts: 3.78 us -> 2.29 us
    pallas_call x1, Pallas kernels: 85.8 us -> 94.5 us  [on_device(): pl.pallas_call(kernel, out_shape=(jax.ShapeDtypeStruct((TOK, HEADS * SIZE...]
    unnamed x4 -> x2, local copies, waits for them, and re-layouts: 3.78 us -> 2.29 us
where the time goes in v5:
time: 97.5 us; the launch traced here: 97.4 us
  Pallas kernels  94.5 us (97%)
  local copies, waits for them, and re-layouts  2.29 us (2%)
    pallas_call x1, Pallas kernels, on_device(): pl.pallas_call(kernel, out_shape=(jax.ShapeDtypeStruct((TOK, HEADS * SIZE...  94.5 us
    unnamed x2, local copies, waits for them, and re-layouts  2.29 us

profile of v5, /device:TPU:1, one launch (start us, length us, event | category | flops | bytes accessed | tf_op | source)
XLA Modules:
  0.0 97.4 jit_solution(10198184192951003359)
XLA Ops:
  0.6 94.5 %attend_and_send.1 = (bf16[256,2048]{1,0:T(8,128)(2,1)S(1)}, bf16[4,2,64,2048]{3,2,1,0:T(8,128)(2,1)S(1)}) custom-call(bf16[256,2048]{1,0:T(8,128)(2,1)} %q_hbm.1, bf16[256,256]{1,0:T(8,128)(2,1)} %k_hbm.1, bf16[256,256]{1,0:T(8,128)(2,1)} %v_hbm.1, s32[1,256]{1,0:T(1,128)} %bitcast.4, s32[1,256]{1,0:T(1,128)} %bitcast.5), custom_call_target="tpu_custom_call" | custom-call | flops 12000000000 | bytes 6000000 | tf_op jit(solution)/shard_map/attend_and_send/pallas_call | solution.py:418
  95.1 1.0 copy.9
  96.1 1.3 %copy.10 = bf16[512,2048]{1,0:T(8,128)(2,1)} copy(bf16[512,2048]{1,0:T(8,128)(2,1)S(1)} %bitcast.3) | data formatting | bytes 4194304

commit v6 on v5

--- a/solution.py
+++ b/solution.py
@@ -17,6 +17,8 @@
 STEP = 4
 KEY_ROW, ALL_ROWS = SIZE + 16, 2 * SIZE + 16
 HIDDEN = 1e30
+GROUP = 4
+WIDE = GROUP * TOK
 TO_LOG2 = SIZE ** -0.5 * 1.4426950408889634
 
 ARRIVALS = (
@@ -206,7 +208,8 @@
         own_values[half, SIZE:KEY_ROW, :] = jnp.where(extra == 0, 1.0, 0.0).astype(BF16)
     inputs[4].wait()
     for h in range(HEADS):
-        q_turned[h] = q_own[:, h * SIZE:(h + 1) * SIZE].astype(F32).T.astype(BF16)
+        turned = q_own[:, h * SIZE:(h + 1) * SIZE].astype(F32).T.astype(BF16)
+        q_turned[h // GROUP, :, (h % GROUP) * TOK:(h % GROUP + 1) * TOK] = turned
     bias[...] = jnp.where((at0 <= at1) & (seg_tall == seg_wide), 0.0, -HIDDEN)
 
     inputs[3].wait()
@@ -298,100 +301,112 @@
 
     scores_of, weights_of = (scores_a, scores_b), (weights_a, weights_b)
     peaks_of, shrink_of = (peaks_a, peaks_b), (shrink_a, shrink_b)
-
-    def score(n, h, slots):
+    first_wide = jnp.concatenate([(seg_row == first_seg).astype(F32)] * GROUP, axis=1)
+
+    def half_of(group):
+        return group // (RATIO // GROUP)
+
+    def score(n, group, slots, c):
+        half = half_of(group)
         if slots is None:
-            keys = k_own[:, (h // RATIO) * SIZE:(h // RATIO + 1) * SIZE]
+            keys = k_own[:, half * SIZE:(half + 1) * SIZE]
         else:
-            keys = jnp.concatenate(
-                [kv[h // RATIO, slot, KEY_ROW:ALL_ROWS, lanes:lanes + SIZE] for slot in slots for lanes in (0, SIZE)], axis=0)
-        product = jnp.dot(keys, q_turned[h], preferred_element_type=F32)
+            keys = jnp.concatenate([kv[half, slots[c], KEY_ROW:ALL_ROWS, lanes:lanes + SIZE] for lanes in (0, SIZE)], axis=0)
+        product = jnp.dot(keys, q_turned[group], preferred_element_type=F32)
         if slots is None:
-            product += bias[...]
-        scores_of[n % 2][0:product.shape[0], :] = product
-        for c in range(product.shape[0] // TOK):
-            peaks_of[n % 2][c] = jnp.max(product[c * TOK:(c + 1) * TOK], axis=0, keepdims=True)
-
-    def peak_rows(n, h, slots):
+            product += jnp.concatenate([bias[...]] * GROUP, axis=1)
+        scores_of[n % 2][c * TOK:(c + 1) * TOK, :] = product
+        peaks_of[n % 2][c] = jnp.max(product, axis=0, keepdims=True)
+
+    def peak_rows(n, group, slots):
         if slots is None:
-            top[h] = peaks_of[n % 2][0]
-            return [top[h]]
+            top[group] = peaks_of[n % 2][0]
+            return [top[group]]
         seen = []
         for slot in slots:
-            block_seg = kv[h // RATIO, slot, SIZE:KEY_ROW, :].astype(F32)[1:2, :]
-            seen.append((block_seg == first_seg) & (seg_row == first_seg))
-        old = top[h]
+            block_seg = kv[half_of(group), slot, SIZE:KEY_ROW, :].astype(F32)[1:2, :]
+            same = jnp.concatenate([(block_seg == first_seg).astype(F32)] * GROUP, axis=1)
+            seen.append(same * first_wide > 0.5)
+        old = top[group]
         peak = old
         for c in range(len(slots)):
             peak = jnp.maximum(peak, jnp.where(seen[c], peaks_of[n % 2][c], -HIDDEN))
-        top[h] = peak
+        top[group] = peak
         shrink_of[n % 2][...] = jnp.exp2((old - peak) * TO_LOG2)
         return [jnp.where(seen[c], peak, HIDDEN) for c in range(len(slots))]
 
-    def soften(n, peaks, c, start, rows):
-        at = slice(c * TOK + start, c * TOK + start + rows)
-        weights_of[n % 2][at, :] = jnp.exp2((scores_of[n % 2][at, :] - peaks[c]) * TO_LOG2).astype(BF16)
-
-    def combine(n, h, slots):
+    def soften(n, peak, c):
+        for at in range(c * TOK, (c + 1) * TOK, 16):
+            rows = slice(at, at + 16)
+            weights_of[n % 2][rows, :] = jnp.exp2((scores_of[n % 2][rows, :] - peak) * TO_LOG2).astype(BF16)
+
+    def combine(n, group, slots, c):
+        values = own_values[half_of(group)] if slots is None else kv[half_of(group), slots[c], 0:KEY_ROW, :]
+        product = jnp.dot(values, weights_of[n % 2][c * TOK:(c + 1) * TOK, :], preferred_element_type=F32)
         if slots is None:
-            acc[h] = jnp.dot(own_values[h // RATIO], weights_of[n % 2][0:TOK, :], preferred_element_type=F32)
+            acc[group] = product
+        elif c == 0:
+            acc[group] = acc[group] * shrink_of[n % 2][...] + product
         else:
-            values = jnp.concatenate([kv[h // RATIO, slot, 0:KEY_ROW, :] for slot in slots], axis=1)
-            product = jnp.dot(values, weights_of[n % 2][...], preferred_element_type=F32)
-            acc[h] = acc[h] * shrink_of[n % 2][...] + product
+            acc[group] += product
 
     def turn(n, before, now, after):
         peaks = peak_rows(n, *now)
-        if before is not None:
-            combine(n - 1, *before)
         for c in range(len(peaks)):
-            if after is not None and c == len(peaks) // 2:
-                score(n + 1, *after)
-            for start in range(0, TOK, 64):
-                soften(n, peaks, c, start, 64)
-
-    for half in range(2):
-        heads = [(half * RATIO + i, None) for i in range(RATIO)]
-        score(0, *heads[0])
-        for n in range(RATIO):
-            turn(n, heads[n - 1] if n > 0 else None, heads[n], heads[n + 1] if n + 1 < RATIO else None)
-        combine(RATIO - 1, *heads[-1])
-        for j in range(4):
-            arrive(0, half, j)
-        if half == 0:
+            if before is not None:
+                combine(n - 1, *before, c)
+            if after is not None:
+                score(n + 1, *after, c)
+            soften(n, peaks[c], c)
+
+    groups = HEADS // GROUP
+    turns = [(group, None) for group in range(groups)]
+    score(0, *turns[0], 0)
+    for n in range(groups):
+        turn(n, turns[n - 1] if n > 0 else None, turns[n], turns[n + 1] if n + 1 < groups else None)
+        for item in (2 * n, 2 * n + 1):
+            arrive(0, item // 4, item % 4)
+        if n == 1:
             first_leg()
+    combine(groups - 1, *turns[-1], 0)
 
     def slots_of(k):
         return [STEP * k + 1 + c for c in range(STEP)]
 
-    score(0, 0, slots_of(0))
+    for c in range(STEP):
+        score(0, 0, slots_of(0), c)
 
     def step(k, carry):
-        now = slots_of(k)
-        turns = [(h, now) for h in range(HEADS)] + [(0, slots_of(jnp.minimum(k + 1, 4)))]
-        for n in range(HEADS):
+        turns = [(group, slots_of(k)) for group in range(groups)] + [(0, slots_of(jnp.minimum(k + 1, 4)))]
+        for n in range(groups):
             turn(n, turns[n - 1] if n > 0 else None, turns[n], turns[n + 1])
-            if n == HEADS - 1:
-                combine(n, *turns[n])
+            if n == groups - 1:
+                for c in range(STEP):
+                    combine(n, *turns[n], c)
+            items = ((0, 1), (2, 3), (4, 5, 6), (7,))[n]
+
+            @pl.when(k < 4)
+            def _():
+                for item in items:
+                    arrive(k + 1, item // 4, item % 4)
+
+            @pl.when(k > 0)
+            def _():
+                for item in items:
+                    drain(k - 1, item % 2, item // 2)
             if n % 2 == 1:
-                @pl.when(k < 4)
+                @pl.when(k == (3, 1)[n // 2])
                 def _():
-                    arrive(k + 1, n // 8, (n // 2) % 4)
-
-                @pl.when(k > 0)
-                def _():
-                    drain(k - 1, n // 8, (n // 2) % 4)
-            if n % 8 == 7:
-                @pl.when(k == (3, 1)[n // 8])
-                def _():
-                    (third_leg, second_leg)[n // 8]()
+                    (third_leg, second_leg)[n // 2]()
         return carry
 
     lax.fori_loop(0, 5, step, 0)
     fourth_leg()
 
     for h in range(HEADS):
-        out_ref[:, h * SIZE:(h + 1) * SIZE] = (acc[h, 0:SIZE, :] * (1.0 / acc[h, SIZE:SIZE + 1, :])).T.astype(BF16)
+        group, lanes = h // GROUP, slice((h % GROUP) * TOK, (h % GROUP + 1) * TOK)
+        attended = acc[group, 0:SIZE, lanes] * (1.0 / acc[group, SIZE:SIZE + 1, lanes])
+        out_ref[:, h * SIZE:(h + 1) * SIZE] = attended.T.astype(BF16)
 
     for half in range(2):
         forward(half, 0, first[half], wait=True)
@@ -425,7 +440,7 @@
         out_specs=(pl.BlockSpec(memory_space=pltpu.VMEM), whole),
         scratch_shapes=[
             pltpu.VMEM((TOK, HEADS * SIZE), BF16),
-            pltpu.VMEM((HEADS, SIZE, TOK), BF16),
+            pltpu.VMEM((HEADS // GROUP, SIZE, WIDE), BF16),
             pltpu.VMEM((TOK, 2 * SIZE), BF16),
             pltpu.VMEM((TOK, 2 * SIZE), BF16),
             pltpu.VMEM((2, KEY_ROW, TOK), BF16),
@@ -433,16 +448,16 @@
             pltpu.VMEM((1, TOK), jnp.int32),
             pltpu.VMEM((2, REACH + 1, ALL_ROWS, TOK), BF16),
             pltpu.VMEM((TOK, TOK), F32),
-            pltpu.VMEM((HEADS, 1, TOK), F32),
-            pltpu.VMEM((HEADS, KEY_ROW, TOK), F32),
-            pltpu.VMEM((STEP * TOK, TOK), F32),
-            pltpu.VMEM((STEP * TOK, TOK), F32),
-            pltpu.VMEM((STEP * TOK, TOK), BF16),
-            pltpu.VMEM((STEP * TOK, TOK), BF16),
-            pltpu.VMEM((STEP, 1, TOK), F32),
-            pltpu.VMEM((STEP, 1, TOK), F32),
-            pltpu.VMEM((1, TOK), F32),
-            pltpu.VMEM((1, TOK), F32),
+            pltpu.VMEM((HEADS // GROUP, 1, WIDE), F32),
+            pltpu.VMEM((HEADS // GROUP, KEY_ROW, WIDE), F32),
+            pltpu.VMEM((STEP * TOK, WIDE), F32),
+            pltpu.VMEM((STEP * TOK, WIDE), F32),
+            pltpu.VMEM((STEP * TOK, WIDE), BF16),
+            pltpu.VMEM((STEP * TOK, WIDE), BF16),
+            pltpu.VMEM((STEP, 1, WIDE), F32),
+            pltpu.VMEM((STEP, 1, WIDE), F32),
+            pltpu.VMEM((1, WIDE), F32),
+            pltpu.VMEM((1, WIDE), F32),
             pltpu.VMEM((4, 2, 8, 2 * SLOT, 2 * SIZE), BF16),
             pltpu.VMEM((8, 4, 2, 2 * SLOT, 2 * SIZE), BF16),
             pltpu.VMEM((4, 8, 2, 2 * SLOT, 2 * SIZE), BF16),

time: 97.5 us -> 97.5 us (level)
  no operation moved by 1% of the time
where the time goes in v6:
time: 97.5 us; the launch traced here: 97.4 us
  Pallas kernels  94.5 us (97%)
  local copies, waits for them, and re-layouts  2.29 us (2%)
    pallas_call x1, Pallas kernels, on_device(): pl.pallas_call(kernel, out_shape=(jax.ShapeDtypeStruct((TOK, HEADS * SIZE...  94.5 us
    unnamed x2, local copies, waits for them, and re-layouts  2.29 us

profile of v6, /device:TPU:1, one launch (start us, length us, event | category | flops | bytes accessed | tf_op | source)
XLA Modules:
  0.0 97.4 jit_solution(13090404031754685334)
XLA Ops:
  0.6 94.5 %attend_and_send.1 = (bf16[256,2048]{1,0:T(8,128)(2,1)S(1)}, bf16[4,2,64,2048]{3,2,1,0:T(8,128)(2,1)S(1)}) custom-call(bf16[256,2048]{1,0:T(8,128)(2,1)} %q_hbm.1, bf16[256,256]{1,0:T(8,128)(2,1)} %k_hbm.1, bf16[256,256]{1,0:T(8,128)(2,1)} %v_hbm.1, s32[1,256]{1,0:T(1,128)} %bitcast.4, s32[1,256]{1,0:T(1,128)} %bitcast.5), custom_call_target="tpu_custom_call" | custom-call | flops 12000000000 | bytes 6000000 | tf_op jit(solution)/shard_map/attend_and_send/pallas_call | solution.py:433
  95.1 1.0 copy.9
  96.1 1.3 %copy.10 = bf16[512,2048]{1,0:T(8,128)(2,1)} copy(bf16[512,2048]{1,0:T(8,128)(2,1)S(1)} %bitcast.3) | data formatting | bytes 4194304

commit v7 on v6

--- a/solution.py
+++ b/solution.py
@@ -17,43 +17,47 @@
 STEP = 4
 KEY_ROW, ALL_ROWS = SIZE + 16, 2 * SIZE + 16
 HIDDEN = 1e30
-GROUP = 4
+GROUP = 2
 WIDE = GROUP * TOK
+
+Z_AFTER = {1: 1, 2: 0, 3: 11, 4: 0, 5: 0, 6: 12, 7: 11}
+X_AFTER = {1: 25, 2: 26, 3: 29}
+Y_AFTER = {2: 38, 1: 38, 0: 35}
 TO_LOG2 = SIZE ** -0.5 * 1.4426950408889634
 
 ARRIVALS = (
-    ((16, 109, 308, 215, 214, 101, 307, 17, 206, 102, 310, 205, 103, 18, 19, 311, 204, 113, 312, 20),
-     (16, 215, 109, 308, 307, 214, 101, 102, 17, 310, 206, 18, 311, 205, 103, 104, 19, 312, 213, 20)),
-    ((101, 16, 215, 17, 308, 110, 207, 309, 102, 306, 18, 213, 212, 305, 103, 104, 19, 311, 20, 214),
-     (16, 101, 308, 215, 17, 309, 110, 207, 214, 102, 306, 103, 18, 19, 205, 311, 213, 104, 312, 20)),
-    ((101, 16, 308, 102, 17, 215, 307, 18, 214, 111, 213, 306, 310, 103, 205, 19, 109, 212, 304, 20),
-     (101, 16, 215, 308, 102, 17, 214, 109, 307, 18, 111, 206, 212, 305, 103, 310, 304, 19, 213, 20)),
-    ((101, 16, 308, 102, 17, 215, 214, 103, 18, 307, 19, 206, 310, 112, 213, 311, 109, 204, 305, 20),
-     (16, 101, 215, 308, 102, 17, 309, 207, 103, 18, 213, 306, 110, 19, 311, 112, 214, 205, 304, 20)),
-    ((101, 16, 215, 308, 102, 17, 309, 103, 18, 207, 214, 104, 19, 310, 305, 111, 20, 212, 306, 213),
-     (16, 101, 215, 308, 102, 17, 214, 309, 103, 18, 306, 204, 110, 19, 213, 305, 107, 20, 212, 311)),
-    ((16, 101, 102, 215, 308, 17, 103, 18, 214, 307, 104, 19, 213, 105, 20, 309, 210, 312, 206, 311),
-     (101, 16, 215, 308, 17, 102, 205, 307, 103, 18, 214, 309, 306, 104, 19, 213, 311, 212, 110, 20)),
-    ((101, 16, 215, 308, 102, 17, 309, 103, 214, 18, 104, 19, 310, 207, 311, 105, 20, 206, 213, 312),
-     (101, 16, 206, 308, 102, 17, 215, 18, 309, 103, 214, 310, 213, 104, 19, 311, 107, 20, 312, 205)),
-    ((16, 207, 101, 308, 215, 102, 17, 309, 103, 18, 310, 104, 214, 19, 213, 20, 306, 111, 212, 305),
-     (207, 101, 16, 102, 17, 308, 309, 215, 103, 18, 214, 19, 310, 111, 306, 104, 213, 305, 20, 212)),
-    ((16, 308, 101, 17, 215, 207, 102, 309, 206, 18, 103, 212, 310, 19, 104, 314, 20, 213, 105, 311),
-     (308, 16, 215, 207, 101, 102, 17, 18, 103, 309, 206, 310, 19, 104, 205, 20, 211, 112, 313, 314)),
-    ((308, 101, 16, 207, 309, 102, 17, 214, 18, 315, 213, 103, 310, 19, 104, 206, 20, 105, 211, 312),
-     (308, 101, 16, 17, 207, 309, 102, 214, 103, 18, 315, 19, 206, 104, 212, 310, 20, 105, 211, 313)),
-    ((308, 101, 16, 215, 309, 17, 102, 214, 310, 103, 18, 19, 207, 104, 212, 311, 20, 105, 206, 313),
-     (308, 101, 16, 102, 215, 309, 17, 18, 207, 310, 103, 213, 104, 19, 212, 314, 20, 105, 311, 206)),
-    ((16, 308, 101, 215, 309, 102, 207, 17, 310, 18, 103, 311, 104, 213, 19, 314, 20, 105, 206, 212),
-     (308, 101, 16, 17, 309, 102, 214, 103, 207, 310, 18, 213, 19, 315, 104, 206, 105, 212, 311, 20)),
-    ((308, 101, 16, 309, 17, 102, 310, 103, 214, 18, 213, 311, 19, 315, 104, 207, 112, 20, 205, 206),
-     (308, 101, 16, 215, 102, 207, 309, 17, 214, 18, 310, 103, 104, 213, 19, 312, 20, 206, 311, 105)),
-    ((308, 101, 16, 102, 215, 309, 17, 214, 310, 18, 103, 206, 311, 104, 19, 207, 312, 20, 105, 213),
-     (101, 16, 308, 215, 309, 17, 102, 103, 214, 310, 18, 19, 207, 311, 104, 105, 213, 312, 20, 206)),
-    ((308, 101, 16, 215, 17, 309, 102, 207, 103, 214, 310, 18, 311, 19, 104, 213, 312, 105, 20, 206),
-     (16, 308, 101, 309, 102, 215, 17, 310, 18, 103, 207, 104, 214, 311, 19, 20, 213, 312, 105, 206)),
-    ((308, 16, 207, 101, 102, 309, 215, 17, 18, 310, 103, 214, 104, 213, 311, 19, 312, 20, 105, 106),
-     (207, 101, 308, 16, 309, 215, 17, 102, 310, 214, 103, 18, 311, 19, 104, 213, 105, 20, 312, 106)),
+    ((16, 215, 308, 109, 214, 307, 101, 206, 102, 213, 17, 305, 18, 310, 212, 311, 204, 103, 20, 19),
+     (16, 308, 109, 215, 301, 110, 214, 17, 307, 102, 213, 306, 205, 103, 18, 112, 19, 304, 211, 20)),
+    ((16, 101, 308, 215, 117, 307, 214, 110, 213, 309, 102, 103, 305, 212, 18, 19, 306, 211, 204, 20),
+     (101, 16, 17, 308, 215, 110, 309, 214, 302, 111, 206, 18, 307, 212, 305, 213, 103, 104, 19, 120)),
+    ((16, 101, 308, 215, 17, 307, 214, 102, 109, 18, 306, 213, 111, 310, 212, 103, 305, 104, 19, 20),
+     (101, 16, 17, 308, 215, 102, 18, 307, 214, 213, 111, 309, 306, 212, 103, 305, 19, 210, 104, 120)),
+    ((16, 101, 308, 215, 17, 102, 307, 214, 18, 103, 309, 213, 110, 19, 205, 112, 311, 206, 104, 120),
+     (101, 16, 17, 308, 215, 102, 309, 214, 18, 103, 306, 213, 19, 310, 212, 311, 104, 305, 207, 20)),
+    ((16, 101, 308, 215, 17, 102, 307, 214, 18, 309, 103, 306, 204, 310, 19, 20, 311, 213, 205, 212),
+     (101, 16, 215, 17, 308, 102, 309, 214, 18, 103, 213, 19, 104, 207, 110, 20, 306, 111, 312, 205)),
+    ((101, 16, 17, 215, 308, 307, 102, 205, 309, 18, 103, 214, 306, 19, 104, 213, 110, 20, 212, 311),
+     (16, 101, 215, 308, 102, 17, 214, 18, 103, 205, 309, 19, 104, 213, 307, 311, 20, 206, 310, 112)),
+    ((101, 16, 308, 17, 206, 102, 18, 309, 215, 307, 103, 310, 214, 19, 104, 213, 311, 212, 20, 105),
+     (16, 101, 215, 308, 17, 307, 206, 102, 103, 18, 214, 19, 104, 310, 209, 311, 20, 105, 312, 213)),
+    ((207, 16, 101, 308, 102, 17, 309, 18, 215, 103, 214, 19, 213, 306, 104, 310, 212, 311, 20, 105),
+     (16, 101, 207, 308, 17, 215, 102, 309, 18, 310, 103, 306, 104, 19, 214, 20, 105, 213, 311, 212)),
+    ((308, 16, 215, 101, 207, 317, 102, 213, 103, 18, 309, 314, 19, 206, 310, 212, 104, 205, 111, 20),
+     (16, 308, 109, 207, 317, 102, 215, 318, 214, 206, 103, 101, 19, 212, 310, 104, 311, 20, 313, 205)),
+    ((16, 308, 101, 215, 109, 17, 214, 102, 207, 213, 318, 103, 104, 19, 206, 310, 20, 311, 212, 205),
+     (308, 101, 16, 17, 309, 215, 110, 207, 318, 103, 213, 319, 206, 314, 104, 212, 102, 20, 311, 105)),
+    ((16, 101, 308, 215, 17, 309, 214, 102, 207, 110, 18, 103, 213, 319, 206, 104, 212, 105, 320, 311),
+     (308, 16, 101, 309, 215, 102, 17, 18, 310, 214, 111, 207, 213, 319, 104, 320, 212, 105, 206, 103)),
+    ((16, 308, 101, 215, 102, 17, 309, 18, 207, 310, 214, 103, 111, 213, 19, 206, 104, 212, 320, 105),
+     (101, 16, 308, 17, 309, 215, 214, 102, 310, 103, 18, 19, 311, 207, 112, 213, 320, 105, 206, 204)),
+    ((16, 308, 101, 215, 17, 309, 214, 102, 207, 103, 18, 310, 19, 213, 311, 104, 206, 312, 20, 205),
+     (101, 16, 308, 215, 17, 309, 102, 18, 310, 207, 103, 311, 214, 104, 19, 20, 206, 112, 205, 113)),
+    ((101, 16, 308, 215, 17, 309, 207, 102, 214, 18, 310, 103, 313, 104, 19, 311, 206, 20, 205, 212),
+     (16, 308, 101, 215, 102, 17, 309, 18, 310, 103, 214, 19, 207, 313, 206, 104, 311, 105, 20, 312)),
+    ((16, 308, 101, 309, 215, 102, 17, 18, 314, 310, 207, 103, 206, 19, 213, 104, 311, 105, 20, 312),
+     (308, 101, 16, 215, 17, 309, 206, 102, 207, 103, 18, 314, 19, 310, 104, 311, 213, 20, 312, 105)),
+    ((308, 101, 16, 207, 17, 215, 309, 102, 310, 103, 214, 18, 19, 311, 220, 104, 312, 213, 105, 106),
+     (16, 207, 308, 101, 309, 102, 17, 215, 18, 214, 310, 103, 104, 19, 311, 20, 312, 213, 105, 106)),
 )
 
 
@@ -259,9 +263,7 @@
     def own_copy():
         return pltpu.make_async_copy(block.at[y], rows_of(y, g), own_sem)
 
-    def first_leg():
-        for by in (1, 7, 2, 6, 3, 5, 4):
-            z_copy(by).start()
+    def keep_first():
         for i in range(4):
             for j in range(2):
                 mid[z, i, j] = outgoing[i, j, z]
@@ -270,8 +272,6 @@
         for by in range(1, 8):
             src = (z + 8 - by) % 8
             pltpu.make_async_copy(mid.at[src], mid.at[src], z_recv.at[src]).wait()
-        for by in (1, 3, 2):
-            x_copy(by).start()
         for i in range(8):
             recv[x, i] = mid[i, x]
 
@@ -288,10 +288,15 @@
                 arrived = recv[src, :, j].reshape(128, 2 * SIZE)
                 block[j, src, :, 0:256] = jnp.dot(key_rows, arrived, preferred_element_type=F32).astype(BF16)
                 block[j, src, :, 256:512] = jnp.dot(value_rows, arrived, preferred_element_type=F32).astype(BF16)
-        for n in range(3):
-            y_copy(n).start()
         c_copy(3).start()
         own_copy().start()
+
+    legs = [(after, z_copy(by).start) for by, after in Z_AFTER.items()]
+    legs += [(min(X_AFTER.values()), second_leg)] + [(after, x_copy(by).start) for by, after in X_AFTER.items()]
+    legs += [(min(Y_AFTER.values()), third_leg)] + [(after, y_copy(n).start) for n, after in Y_AFTER.items()]
+
+    def legs_at(count):
+        return [start for after, start in legs if after == count]
 
     def fourth_leg():
         for n in range(3):
@@ -361,13 +366,15 @@
 
     groups = HEADS // GROUP
     turns = [(group, None) for group in range(groups)]
+    for start in legs_at(0):
+        start()
+    keep_first()
     score(0, *turns[0], 0)
     for n in range(groups):
         turn(n, turns[n - 1] if n > 0 else None, turns[n], turns[n + 1] if n + 1 < groups else None)
-        for item in (2 * n, 2 * n + 1):
-            arrive(0, item // 4, item % 4)
-        if n == 1:
-            first_leg()
+        arrive(0, n // 4, n % 4)
+        for start in legs_at(n + 1):
+            start()
     combine(groups - 1, *turns[-1], 0)
 
     def slots_of(k):
@@ -383,21 +390,22 @@
             if n == groups - 1:
                 for c in range(STEP):
                     combine(n, *turns[n], c)
-            items = ((0, 1), (2, 3), (4, 5, 6), (7,))[n]
 
             @pl.when(k < 4)
             def _():
-                for item in items:
-                    arrive(k + 1, item // 4, item % 4)
+                arrive(k + 1, n // 4, n % 4)
 
             @pl.when(k > 0)
             def _():
-                for item in items:
-                    drain(k - 1, item % 2, item // 2)
-            if n % 2 == 1:
-                @pl.when(k == (3, 1)[n // 2])
-                def _():
-                    (third_leg, second_leg)[n // 2]()
+                drain(k - 1, n % 2, n // 2)
+
+            for at in range(4):
+                starts = legs_at(8 * (at + 1) + n + 1)
+                if starts:
+                    @pl.when(k == at)
+                    def _():
+                        for start in starts:
+                            start()
         return carry
 
     lax.fori_loop(0, 5, step, 0)

time: 97.5 us -> 84.9 us (0.87)
  Pallas kernels: 94.5 us -> 81.9 us
    pallas_call x1, Pallas kernels: 94.5 us -> 81.9 us  [on_device(): pl.pallas_call(kernel, out_shape=(jax.ShapeDtypeStruct((TOK, HEADS * SIZE...]
where the time goes in v7:
time: 84.9 us; the launch traced here: 84.8 us
  Pallas kernels  81.9 us (96%)
  local copies, waits for them, and re-layouts  2.29 us (3%)
    pallas_call x1, Pallas kernels, on_device(): pl.pallas_call(kernel, out_shape=(jax.ShapeDtypeStruct((TOK, HEADS * SIZE...  81.9 us
    unnamed x2, local copies, waits for them, and re-layouts  2.29 us

profile of v7, /device:TPU:1, one launch (start us, length us, event | category | flops | bytes accessed | tf_op | source)
XLA Modules:
  0.0 84.8 jit_solution(15066388612484630729)
XLA Ops:
  0.6 81.9 %attend_and_send.1 = (bf16[256,2048]{1,0:T(8,128)(2,1)S(1)}, bf16[4,2,64,2048]{3,2,1,0:T(8,128)(2,1)S(1)}) custom-call(bf16[256,2048]{1,0:T(8,128)(2,1)} %q_hbm.1, bf16[256,256]{1,0:T(8,128)(2,1)} %k_hbm.1, bf16[256,256]{1,0:T(8,128)(2,1)} %v_hbm.1, s32[1,256]{1,0:T(1,128)} %bitcast.4, s32[1,256]{1,0:T(1,128)} %bitcast.5), custom_call_target="tpu_custom_call" | custom-call | flops 12000000000 | bytes 6000000 | tf_op jit(solution)/shard_map/attend_and_send/pallas_call | solution.py:441
  82.6 1.0 %copy.9 = bf16[256,2048]{1,0:T(8,128)(2,1)} copy(bf16[256,2048]{1,0:T(8,128)(2,1)S(1)} %get-tuple-element.8) | data formatting | bytes 2097152
  83.5 1.3 %copy.10 = bf16[512,2048]{1,0:T(8,128)(2,1)} copy(bf16[512,2048]{1,0:T(8,128)(2,1)S(1)} %bitcast.3) | data formatting | bytes 4194304

commit v8 on v7

--- a/solution.py
+++ b/solution.py
@@ -20,44 +20,44 @@
 GROUP = 2
 WIDE = GROUP * TOK
 
-Z_AFTER = {1: 1, 2: 0, 3: 11, 4: 0, 5: 0, 6: 12, 7: 11}
-X_AFTER = {1: 25, 2: 26, 3: 29}
-Y_AFTER = {2: 38, 1: 38, 0: 35}
+Z_AFTER = {7: 0, 1: 0, 5: 0, 3: 0, 6: 4, 4: 4, 2: 9}
+X_AFTER = {2: 18, 1: 21, 3: 22}
+Y_AFTER = {0: 30, 1: 32, 2: 33}
 TO_LOG2 = SIZE ** -0.5 * 1.4426950408889634
 
 ARRIVALS = (
-    ((16, 215, 308, 109, 214, 307, 101, 206, 102, 213, 17, 305, 18, 310, 212, 311, 204, 103, 20, 19),
-     (16, 308, 109, 215, 301, 110, 214, 17, 307, 102, 213, 306, 205, 103, 18, 112, 19, 304, 211, 20)),
-    ((16, 101, 308, 215, 117, 307, 214, 110, 213, 309, 102, 103, 305, 212, 18, 19, 306, 211, 204, 20),
-     (101, 16, 17, 308, 215, 110, 309, 214, 302, 111, 206, 18, 307, 212, 305, 213, 103, 104, 19, 120)),
-    ((16, 101, 308, 215, 17, 307, 214, 102, 109, 18, 306, 213, 111, 310, 212, 103, 305, 104, 19, 20),
-     (101, 16, 17, 308, 215, 102, 18, 307, 214, 213, 111, 309, 306, 212, 103, 305, 19, 210, 104, 120)),
-    ((16, 101, 308, 215, 17, 102, 307, 214, 18, 103, 309, 213, 110, 19, 205, 112, 311, 206, 104, 120),
-     (101, 16, 17, 308, 215, 102, 309, 214, 18, 103, 306, 213, 19, 310, 212, 311, 104, 305, 207, 20)),
-    ((16, 101, 308, 215, 17, 102, 307, 214, 18, 309, 103, 306, 204, 310, 19, 20, 311, 213, 205, 212),
-     (101, 16, 215, 17, 308, 102, 309, 214, 18, 103, 213, 19, 104, 207, 110, 20, 306, 111, 312, 205)),
-    ((101, 16, 17, 215, 308, 307, 102, 205, 309, 18, 103, 214, 306, 19, 104, 213, 110, 20, 212, 311),
-     (16, 101, 215, 308, 102, 17, 214, 18, 103, 205, 309, 19, 104, 213, 307, 311, 20, 206, 310, 112)),
-    ((101, 16, 308, 17, 206, 102, 18, 309, 215, 307, 103, 310, 214, 19, 104, 213, 311, 212, 20, 105),
-     (16, 101, 215, 308, 17, 307, 206, 102, 103, 18, 214, 19, 104, 310, 209, 311, 20, 105, 312, 213)),
-    ((207, 16, 101, 308, 102, 17, 309, 18, 215, 103, 214, 19, 213, 306, 104, 310, 212, 311, 20, 105),
-     (16, 101, 207, 308, 17, 215, 102, 309, 18, 310, 103, 306, 104, 19, 214, 20, 105, 213, 311, 212)),
-    ((308, 16, 215, 101, 207, 317, 102, 213, 103, 18, 309, 314, 19, 206, 310, 212, 104, 205, 111, 20),
-     (16, 308, 109, 207, 317, 102, 215, 318, 214, 206, 103, 101, 19, 212, 310, 104, 311, 20, 313, 205)),
-    ((16, 308, 101, 215, 109, 17, 214, 102, 207, 213, 318, 103, 104, 19, 206, 310, 20, 311, 212, 205),
-     (308, 101, 16, 17, 309, 215, 110, 207, 318, 103, 213, 319, 206, 314, 104, 212, 102, 20, 311, 105)),
-    ((16, 101, 308, 215, 17, 309, 214, 102, 207, 110, 18, 103, 213, 319, 206, 104, 212, 105, 320, 311),
-     (308, 16, 101, 309, 215, 102, 17, 18, 310, 214, 111, 207, 213, 319, 104, 320, 212, 105, 206, 103)),
-    ((16, 308, 101, 215, 102, 17, 309, 18, 207, 310, 214, 103, 111, 213, 19, 206, 104, 212, 320, 105),
-     (101, 16, 308, 17, 309, 215, 214, 102, 310, 103, 18, 19, 311, 207, 112, 213, 320, 105, 206, 204)),
-    ((16, 308, 101, 215, 17, 309, 214, 102, 207, 103, 18, 310, 19, 213, 311, 104, 206, 312, 20, 205),
-     (101, 16, 308, 215, 17, 309, 102, 18, 310, 207, 103, 311, 214, 104, 19, 20, 206, 112, 205, 113)),
-    ((101, 16, 308, 215, 17, 309, 207, 102, 214, 18, 310, 103, 313, 104, 19, 311, 206, 20, 205, 212),
-     (16, 308, 101, 215, 102, 17, 309, 18, 310, 103, 214, 19, 207, 313, 206, 104, 311, 105, 20, 312)),
-    ((16, 308, 101, 309, 215, 102, 17, 18, 314, 310, 207, 103, 206, 19, 213, 104, 311, 105, 20, 312),
-     (308, 101, 16, 215, 17, 309, 206, 102, 207, 103, 18, 314, 19, 310, 104, 311, 213, 20, 312, 105)),
-    ((308, 101, 16, 207, 17, 215, 309, 102, 310, 103, 214, 18, 19, 311, 220, 104, 312, 213, 105, 106),
-     (16, 207, 308, 101, 309, 102, 17, 215, 18, 214, 310, 103, 104, 19, 311, 20, 312, 213, 105, 106)),
+    ((215, 109, 101, 16, 206, 307, 308, 205, 102, 310, 18, 213, 17, 111, 204, 203, 214, 20, 19, 112),
+     (109, 215, 207, 301, 102, 110, 103, 206, 17, 16, 308, 214, 19, 205, 111, 304, 18, 213, 20, 112)),
+    ((101, 16, 307, 213, 110, 215, 206, 102, 205, 17, 308, 214, 309, 204, 312, 18, 20, 111, 303, 219),
+     (101, 16, 308, 110, 307, 214, 17, 302, 103, 215, 111, 19, 206, 304, 309, 305, 213, 212, 18, 120)),
+    ((16, 101, 214, 102, 307, 206, 215, 103, 305, 111, 309, 19, 17, 204, 213, 208, 110, 20, 312, 18),
+     (16, 101, 102, 215, 308, 214, 307, 309, 306, 104, 213, 17, 18, 112, 303, 305, 120, 110, 219, 211)),
+    ((101, 215, 207, 16, 102, 306, 103, 108, 18, 214, 305, 213, 309, 104, 112, 120, 311, 19, 17, 210),
+     (101, 16, 215, 102, 17, 103, 18, 214, 309, 308, 306, 307, 311, 304, 212, 20, 113, 210, 105, 19)),
+    ((16, 101, 308, 17, 215, 102, 103, 104, 214, 19, 306, 309, 311, 307, 205, 113, 110, 18, 312, 120),
+     (101, 16, 215, 17, 102, 103, 213, 18, 19, 206, 204, 311, 214, 109, 312, 20, 205, 207, 108, 210)),
+    ((16, 101, 102, 206, 215, 103, 308, 310, 17, 19, 104, 205, 211, 120, 307, 218, 109, 112, 114, 213),
+     (16, 102, 214, 101, 307, 215, 205, 104, 218, 309, 208, 311, 306, 20, 17, 119, 203, 112, 113, 310)),
+    ((101, 102, 16, 207, 308, 17, 215, 206, 303, 104, 212, 19, 305, 310, 111, 18, 214, 120, 213, 109),
+     (101, 215, 103, 16, 307, 19, 206, 102, 17, 309, 308, 310, 18, 105, 204, 213, 112, 214, 211, 20)),
+    ((16, 101, 102, 308, 207, 103, 309, 18, 213, 306, 215, 212, 214, 19, 310, 17, 304, 105, 111, 220),
+     (16, 101, 207, 17, 309, 310, 102, 214, 103, 18, 104, 305, 213, 308, 215, 119, 212, 306, 20, 211)),
+    ((16, 215, 207, 101, 308, 103, 102, 213, 19, 18, 314, 206, 104, 17, 205, 111, 309, 112, 210, 20),
+     (308, 16, 109, 207, 214, 317, 102, 206, 315, 311, 103, 310, 18, 212, 101, 104, 19, 105, 20, 213)),
+    ((16, 101, 308, 215, 214, 206, 17, 104, 309, 207, 102, 313, 20, 211, 103, 318, 105, 19, 210, 112),
+     (16, 308, 101, 215, 110, 207, 117, 213, 318, 103, 309, 212, 311, 214, 319, 104, 20, 105, 206, 202)),
+    ((16, 101, 215, 102, 207, 308, 213, 314, 17, 212, 204, 209, 103, 311, 20, 110, 205, 319, 18, 106),
+     (16, 101, 215, 117, 308, 102, 214, 309, 111, 213, 104, 207, 310, 312, 203, 120, 205, 206, 118, 19)),
+    ((16, 308, 101, 102, 214, 215, 213, 17, 205, 103, 310, 311, 309, 206, 19, 207, 104, 118, 212, 20),
+     (16, 101, 215, 102, 17, 309, 214, 103, 308, 19, 310, 206, 112, 204, 207, 105, 20, 113, 18, 111)),
+    ((16, 101, 215, 17, 214, 102, 206, 103, 207, 19, 308, 104, 209, 18, 311, 112, 20, 213, 210, 105),
+     (101, 16, 102, 215, 18, 308, 207, 309, 103, 104, 214, 19, 205, 206, 120, 311, 17, 312, 213, 310)),
+    ((16, 101, 215, 207, 308, 310, 102, 103, 18, 104, 311, 314, 309, 213, 212, 206, 105, 19, 17, 120),
+     (101, 16, 17, 310, 308, 215, 102, 103, 206, 207, 19, 104, 214, 313, 312, 105, 309, 211, 118, 20)),
+    ((16, 308, 101, 102, 18, 17, 111, 213, 103, 314, 207, 215, 210, 309, 105, 312, 104, 320, 106, 219),
+     (16, 101, 308, 215, 207, 217, 102, 314, 311, 18, 103, 209, 310, 104, 206, 212, 105, 113, 20, 19)),
+    ((308, 16, 309, 101, 310, 207, 17, 214, 311, 103, 102, 112, 118, 104, 19, 320, 213, 105, 106, 215),
+     (101, 16, 102, 17, 18, 308, 309, 214, 207, 310, 315, 213, 311, 103, 312, 105, 104, 106, 19, 20)),
 )
 
 
@@ -195,9 +195,9 @@
         keys = jnp.where(seg_tall[:, 0:SIZE] == last_seg[:, 0:SIZE], keys, last_key).astype(BF16)
         kv[half, 0, KEY_ROW:ALL_ROWS, 0:SIZE] = keys[0:SIZE]
         kv[half, 0, KEY_ROW:ALL_ROWS, SIZE:TOK] = keys[SIZE:TOK]
-    pl.semaphore_wait(barrier, len(partners))
-    forward(0, 0, first[0])
-    forward(1, 0, first[1])
+        if half == 0:
+            pl.semaphore_wait(barrier, len(partners))
+        forward(half, 0, first[half])
 
     codes = [
         [
@@ -383,15 +383,20 @@
     for c in range(STEP):
         score(0, 0, slots_of(0), c)
 
+    def start_legs(count):
+        for start in legs_at(count):
+            start()
+
     def step(k, carry):
-        turns = [(group, slots_of(k)) for group in range(groups)] + [(0, slots_of(jnp.minimum(k + 1, 4)))]
+        ahead = [jnp.minimum(STEP * (k + 1) + 1 + c, 18) for c in range(STEP)]
+        turns = [(group, slots_of(k)) for group in range(groups)] + [(0, ahead)]
         for n in range(groups):
             turn(n, turns[n - 1] if n > 0 else None, turns[n], turns[n + 1])
             if n == groups - 1:
                 for c in range(STEP):
                     combine(n, *turns[n], c)
 
-            @pl.when(k < 4)
+            @pl.when(k < 3)
             def _():
                 arrive(k + 1, n // 4, n % 4)
 
@@ -399,16 +404,41 @@
             def _():
                 drain(k - 1, n % 2, n // 2)
 
-            for at in range(4):
-                starts = legs_at(8 * (at + 1) + n + 1)
-                if starts:
+            for at in range(3):
+                if legs_at(8 * (at + 1) + n + 1):
                     @pl.when(k == at)
                     def _():
-                        for start in starts:
-                            start()
+                        start_legs(8 * (at + 1) + n + 1)
+
+            @pl.when(k == 3)
+            def _():
+                if n % 2 == 1:
+                    arrive(4, 0, n // 2)
+                    start_legs(33 + n // 2)
+                drain(3, n % 2, n // 2)
+                if n == groups - 2:
+                    for half in range(2):
+                        forward(half, 0, first[half], wait=True)
+                    for by in range(1, 8):
+                        z_copy(by).wait_send()
         return carry
 
-    lax.fori_loop(0, 5, step, 0)
+    def short_step(m, carry):
+        turns = [(group, [17 + 2 * m, 18 + 2 * m]) for group in range(groups)] + [(0, [19, 20])]
+        for n in range(groups):
+            turn(n, turns[n - 1] if n > 0 else None, turns[n], turns[n + 1])
+            if n == groups - 1:
+                for c in range(2):
+                    combine(n, *turns[n], c)
+            if n % 2 == 1:
+                @pl.when(m == 0)
+                def _():
+                    arrive(4, 1, n // 2)
+                    start_legs(37 + n // 2)
+        return carry
+
+    lax.fori_loop(0, 4, step, 0)
+    lax.fori_loop(0, 2, short_step, 0)
     fourth_leg()
 
     for h in range(HEADS):
@@ -417,11 +447,8 @@
         out_ref[:, h * SIZE:(h + 1) * SIZE] = attended.T.astype(BF16)
 
     for half in range(2):
-        forward(half, 0, first[half], wait=True)
         for jj in range(STEP):
             drain(4, half, jj)
-    for by in range(1, 8):
-        z_copy(by).wait_send()
     for by in range(1, 4):
         x_copy(by).wait_send()
     for n in range(3):

time: 84.9 us -> 91.2 us (1.074)
  Pallas kernels: 81.9 us -> 88.1 us
    pallas_call x1, Pallas kernels: 81.9 us -> 88.1 us  [on_device(): pl.pallas_call(kernel, out_shape=(jax.ShapeDtypeStruct((TOK, HEADS * SIZE...]
where the time goes in v8:
time: 91.2 us; the launch traced here: 91.1 us
  Pallas kernels  88.1 us (97%)
  local copies, waits for them, and re-layouts  2.29 us (3%)
    pallas_call x1, Pallas kernels, on_device(): pl.pallas_call(kernel, out_shape=(jax.ShapeDtypeStruct((TOK, HEADS * SIZE...  88.1 us
    unnamed x2, local copies, waits for them, and re-layouts  2.29 us

profile of v8, /device:TPU:1, one launch (start us, length us, event | category | flops | bytes accessed | tf_op | source)
XLA Modules:
  0.0 91.1 jit_solution(13655728844508348857)
XLA Ops:
  0.6 88.1 %attend_and_send.1 = (bf16[256,2048]{1,0:T(8,128)(2,1)S(1)}, bf16[4,2,64,2048]{3,2,1,0:T(8,128)(2,1)S(1)}) custom-call(bf16[256,2048]{1,0:T(8,128)(2,1)} %q_hbm.1, bf16[256,256]{1,0:T(8,128)(2,1)} %k_hbm.1, bf16[256,256]{1,0:T(8,128)(2,1)} %v_hbm.1, s32[1,256]{1,0:T(1,128)} %bitcast.4, s32[1,256]{1,0:T(1,128)} %bitcast.5), custom_call_target="tpu_custom_call" | custom-call | flops 12000000000 | bytes 6000000 | tf_op jit(solution)/shard_map/attend_and_send/pallas_call | solution.py:468
  88.8 1.0 %copy.9 = bf16[256,2048]{1,0:T(8,128)(2,1)} copy(bf16[256,2048]{1,0:T(8,128)(2,1)S(1)} %get-tuple-element.8) | data formatting | bytes 2097152
  89.8 1.3 %copy.10 = bf16[512,2048]{1,0:T(8,128)(2,1)} copy(bf16[512,2048]{1,0:T(8,128)(2,1)S(1)} %bitcast.3) | data formatting | bytes 4194304

commit v9 on v7

--- a/solution.py
+++ b/solution.py
@@ -20,9 +20,9 @@
 GROUP = 2
 WIDE = GROUP * TOK
 
-Z_AFTER = {1: 1, 2: 0, 3: 11, 4: 0, 5: 0, 6: 12, 7: 11}
+Z_AFTER = {2: 0, 5: 0, 4: 0, 1: 1, 7: 11, 3: 11, 6: 12}
 X_AFTER = {1: 25, 2: 26, 3: 29}
-Y_AFTER = {2: 38, 1: 38, 0: 35}
+Y_AFTER = {0: 35, 2: 38, 1: 38}
 TO_LOG2 = SIZE ** -0.5 * 1.4426950408889634
 
 ARRIVALS = (
@@ -195,9 +195,9 @@
         keys = jnp.where(seg_tall[:, 0:SIZE] == last_seg[:, 0:SIZE], keys, last_key).astype(BF16)
         kv[half, 0, KEY_ROW:ALL_ROWS, 0:SIZE] = keys[0:SIZE]
         kv[half, 0, KEY_ROW:ALL_ROWS, SIZE:TOK] = keys[SIZE:TOK]
-    pl.semaphore_wait(barrier, len(partners))
-    forward(0, 0, first[0])
-    forward(1, 0, first[1])
+        if half == 0:
+            pl.semaphore_wait(barrier, len(partners))
+        forward(half, 0, first[half])
 
     codes = [
         [
@@ -395,9 +395,18 @@
             def _():
                 arrive(k + 1, n // 4, n % 4)
 
-            @pl.when(k > 0)
+            @pl.when((k > 0) & (k < 4))
             def _():
                 drain(k - 1, n % 2, n // 2)
+
+            @pl.when(k == 3)
+            def _():
+                drain(3, n % 2, n // 2)
+                if n == groups - 2:
+                    for half in range(2):
+                        forward(half, 0, first[half], wait=True)
+                    for by in range(1, 8):
+                        z_copy(by).wait_send()
 
             for at in range(4):
                 starts = legs_at(8 * (at + 1) + n + 1)
@@ -417,11 +426,8 @@
         out_ref[:, h * SIZE:(h + 1) * SIZE] = attended.T.astype(BF16)
 
     for half in range(2):
-        forward(half, 0, first[half], wait=True)
         for jj in range(STEP):
             drain(4, half, jj)
-    for by in range(1, 8):
-        z_copy(by).wait_send()
     for by in range(1, 4):
         x_copy(by).wait_send()
     for n in range(3):

time: 84.9 us -> 84.7 us (level)
  no operation moved by 1% of the time
where the time goes in v9:
time: 84.7 us; the launch traced here: 84.6 us
  Pallas kernels  81.7 us (96%)
  local copies, waits for them, and re-layouts  2.29 us (3%)
    pallas_call x1, Pallas kernels, on_device(): pl.pallas_call(kernel, out_shape=(jax.ShapeDtypeStruct((TOK, HEADS * SIZE...  81.7 us
    unnamed x2, local copies, waits for them, and re-layouts  2.29 us

profile of v9, /device:TPU:1, one launch (start us, length us, event | category | flops | bytes accessed | tf_op | source)
XLA Modules:
  0.0 84.6 jit_solution(604440042052321670)
XLA Ops:
  0.6 81.7 %attend_and_send.1 = (bf16[256,2048]{1,0:T(8,128)(2,1)S(1)}, bf16[4,2,64,2048]{3,2,1,0:T(8,128)(2,1)S(1)}) custom-call(bf16[256,2048]{1,0:T(8,128)(2,1)} %q_hbm.1, bf16[256,256]{1,0:T(8,128)(2,1)} %k_hbm.1, bf16[256,256]{1,0:T(8,128)(2,1)} %v_hbm.1, s32[1,256]{1,0:T(1,128)} %bitcast.4, s32[1,256]{1,0:T(1,128)} %bitcast.5), custom_call_target="tpu_custom_call" | custom-call | flops 12000000000 | bytes 6000000 | tf_op jit(solution)/shard_map/attend_and_send/pallas_call | solution.py:447
  82.4 1.0 %copy.9 = bf16[256,2048]{1,0:T(8,128)(2,1)} copy(bf16[256,2048]{1,0:T(8,128)(2,1)S(1)} %get-tuple-element.8) | data formatting | bytes 2097152
  83.3 1.3 %copy.10 = bf16[512,2048]{1,0:T(8,128)(2,1)} copy(bf16[512,2048]{1,0:T(8,128)(2,1)S(1)} %bitcast.3) | data formatting | bytes 4194304
